TPU v7x, 32 devices: a whole 2x2x4 slice. The times are simulated.
32 devices in a mesh: rows: 8 (over z, x), seq: 4 (over y, core).
Axes of the slice: x: 2, y: 2, z: 4, core: 2. Of those that a mesh axis runs over, the one named last changes fastest.
Arguments:
- tokens: bfloat16 [32, 1024, 1024], P('rows', 'seq'), may hold values from -6 to 6
- segment_ids: int32 [32, 1024], P('rows'), may hold values from 0 to 1024, as said below
- grad_out: bfloat16 [32, 1024, 1024], P('rows', 'seq'), may hold values from -6 to 6
- norm1_gain: float32 [1024], replicated, may hold values from 0.1 to 1.9
- norm1_shift: float32 [1024], replicated, may hold values from -1.5 to 1.5
- w_query: bfloat16 [1024, 1024], replicated, may hold values from -0.1875 to 0.1875
- b_query: float32 [1024], replicated, may hold values from -1.5 to 1.5
- w_key: bfloat16 [1024, 1024], replicated, may hold values from -0.1875 to 0.1875
- w_value: bfloat16 [1024, 1024], replicated, may hold values from -0.1875 to 0.1875
- b_value: float32 [1024], replicated, may hold values from -1.5 to 1.5
- w_out: bfloat16 [1024, 1024], replicated, may hold values from -0.75 to 0.75
- b_out: float32 [1024], replicated, may hold values from -1.5 to 1.5
- norm2_gain: float32 [1024], replicated, may hold values from 0.1 to 1.9
- norm2_shift: float32 [1024], replicated, may hold values from -1.5 to 1.5
- w_up: bfloat16 [1024, 4096], replicated, may hold values from -0.1875 to 0.1875
- b_up: float32 [4096], replicated, may hold values from -1.5 to 1.5
- w_down: bfloat16 [4096, 1024], replicated, may hold values from -0.09375 to 0.09375
- b_down: float32 [1024], replicated, may hold values from -1.5 to 1.5
Outputs:
- block_out: bfloat16 [32, 1024, 1024], P('rows', 'seq')
- grad_tokens: bfloat16 [32, 1024, 1024], P('rows', 'seq')
- grad_norm1_gain: float32 [1024], P(('rows', 'seq'))
- grad_norm1_shift: float32 [1024], P(('rows', 'seq'))
- grad_w_query: float32 [1024, 1024], P(('rows', 'seq'))
- grad_b_query: float32 [1024], P(('rows', 'seq'))
- grad_w_key: float32 [1024, 1024], P(('rows', 'seq'))
- grad_w_value: float32 [1024, 1024], P(('rows', 'seq'))
- grad_b_value: float32 [1024], P(('rows', 'seq'))
- grad_w_out: float32 [1024, 1024], P(('rows', 'seq'))
- grad_b_out: float32 [1024], P(('rows', 'seq'))
- grad_norm2_gain: float32 [1024], P(('rows', 'seq'))
- grad_norm2_shift: float32 [1024], P(('rows', 'seq'))
- grad_w_up: float32 [1024, 4096], P(('rows', 'seq'))
- grad_b_up: float32 [4096], P(('rows', 'seq'))
- grad_w_down: float32 [4096, 1024], P(('rows', 'seq'))
- grad_b_down: float32 [1024], P(('rows', 'seq'))
Inputs may be any that keep to these rules, and one draw needn't show every extreme that they name: `segment_ids`: image id of each token; along a row the ids never decrease; the row ends in padding, a run of one or more tokens that hold 1024. A token attends to the tokens of its row with the same id.
All inputs are finite; a program needn't handle non-finite values.
Results may differ from a plain program's by a relative error of at most 0.02.
Values may be sent and summed in bfloat16 or wider, within the bound.
No kernel may reach another device: no remote copies, remote signals or barrier semaphores. Data moves between devices by JAX's collectives and lax.ppermute only.
A program may use at most 320 MiB of HBM per device.

v0:
```python
import jax
import jax.numpy as jnp
from jax import lax
from jax.sharding import PartitionSpec as P

HEADS = 16


norm_eps = 1e-06
masked_score = -1e30


def layer_norm(values, norm_gain, norm_shift):
    row_mean = jnp.mean(values, axis=-1, keepdims=True)
    centered = values - row_mean
    variance = jnp.mean(centered * centered, axis=-1, keepdims=True)
    return centered * lax.rsqrt(variance + norm_eps) * norm_gain + norm_shift


def exact_gelu(values):
    return jax.nn.gelu(values, approximate=False)


def project(left_side, matrix):
    return jnp.dot(left_side, matrix, preferred_element_type=jnp.float32)


def project_back(left_side, matrix):
    return lax.dot_general(
        left_side, matrix, (((1,), (1,)), ((), ())), preferred_element_type=jnp.float32
    )


def weight_grad(inputs, gradients):
    return lax.dot_general(
        inputs, gradients, (((0,), (0,)), ((), ())), preferred_element_type=jnp.float32
    )


def column_sum(values):
    return jnp.sum(values.astype(jnp.float32), axis=0)


def to_groups(values, row_count, length, group_count):
    return jnp.transpose(
        values.reshape(row_count, length, group_count, values.shape[-1] // group_count),
        (2, 0, 1, 3),
    )


def from_groups(values):
    group_count, row_count, length, width = values.shape
    return jnp.transpose(values, (1, 2, 0, 3)).reshape(row_count, length, group_count * width)


def split_heads(values):
    row_count, length, width = values.shape
    return values.reshape(row_count, length, 2, width // 2)


def attend_scores(query_pair, key_pair, same_image, score_scale):
    raw_scores = (
        jnp.einsum(
            "rqhe,rkhe->rhqk",
            split_heads(query_pair),
            split_heads(key_pair),
            preferred_element_type=jnp.float32,
        )
        * score_scale
    )
    return jnp.where(same_image, raw_scores, masked_score)


def probs_and_grads(
    query_pair, key_pair, value_pair, grad_pair, same_image, row_top, row_total, score_scale
):
    scores = attend_scores(query_pair, key_pair, same_image, score_scale)
    probs = jnp.exp(scores - row_top) / row_total
    prob_grad = jnp.einsum(
        "rqhe,rkhe->rhqk",
        split_heads(grad_pair),
        split_heads(value_pair),
        preferred_element_type=jnp.float32,
    )
    return (probs, prob_grad)


def on_device(
    tokens,
    segment_ids,
    grad_out,
    norm1_gain,
    norm1_shift,
    w_query,
    b_query,
    w_key,
    w_value,
    b_value,
    w_out,
    b_out,
    norm2_gain,
    norm2_shift,
    w_up,
    b_up,
    w_down,
    b_down,
):
    row_count, local_len, model_width = tokens.shape
    full_len = segment_ids.shape[1]
    head_dim = model_width // HEADS
    group_count = HEADS // 2
    score_scale = head_dim ** (-0.5)
    token_count = row_count * local_len
    first_token = lax.axis_index("seq") * local_len
    local_ids = lax.dynamic_slice_in_dim(segment_ids, first_token, local_len, 1)
    same_image = (local_ids[:, :, None] == segment_ids[:, None, :])[:, None]
    is_image = (local_ids != full_len).astype(jnp.float32).reshape(token_count, 1)
    inputs = tokens.astype(jnp.float32).reshape(token_count, model_width)
    normed_full, norm1_back = jax.vjp(layer_norm, inputs, norm1_gain, norm1_shift)
    normed = normed_full.astype(jnp.bfloat16)
    queries = (project(normed, w_query) + b_query).astype(jnp.bfloat16)
    key_local = (
        project(normed, w_key).astype(jnp.bfloat16).reshape(row_count, local_len, model_width)
    )
    value_local = (
        (project(normed, w_value) + b_value)
        .astype(jnp.bfloat16)
        .reshape(row_count, local_len, model_width)
    )
    key_rows, value_rows = (
        lax.all_gather(key_local, "seq", axis=1, tiled=True),
        lax.all_gather(value_local, "seq", axis=1, tiled=True),
    )
    query_groups = to_groups(
        queries.reshape(row_count, local_len, model_width), row_count, local_len, group_count
    )
    key_groups = to_groups(key_rows, row_count, full_len, group_count)
    value_groups = to_groups(value_rows, row_count, full_len, group_count)

    def forward_pair(items):
        query_pair, key_pair, value_pair = items
        scores = attend_scores(query_pair, key_pair, same_image, score_scale)
        row_top = jnp.max(scores, axis=-1, keepdims=True)
        exponent = jnp.exp(scores - row_top)
        row_total = jnp.sum(exponent, axis=-1, keepdims=True)
        probs_low = (exponent / row_total).astype(jnp.bfloat16)
        mixed = jnp.einsum(
            "rhqk,rkhe->rqhe",
            probs_low,
            split_heads(value_pair),
            preferred_element_type=jnp.float32,
        )
        return (mixed.astype(jnp.bfloat16).reshape(query_pair.shape), row_top, row_total)

    mixed_groups, top_groups, total_groups = lax.map(
        forward_pair, (query_groups, key_groups, value_groups)
    )
    attended = from_groups(mixed_groups).reshape(token_count, model_width)
    residual = inputs + project(attended, w_out) + b_out
    normed_two_full, norm2_back = jax.vjp(layer_norm, residual, norm2_gain, norm2_shift)
    normed_two = normed_two_full.astype(jnp.bfloat16)
    hidden_pre = project(normed_two, w_up) + b_up
    activated_full, gelu_back = jax.vjp(exact_gelu, hidden_pre)
    activated = activated_full.astype(jnp.bfloat16)
    block_out = residual + project(activated, w_down) + b_down
    out_grad = grad_out.astype(jnp.float32).reshape(token_count, model_width) * is_image
    down_in = out_grad.astype(jnp.bfloat16)
    grad_w_down = weight_grad(activated, down_in)
    grad_b_down = column_sum(down_in)
    hidden_grad = gelu_back(project_back(down_in, w_down))[0].astype(jnp.bfloat16)
    grad_w_up = weight_grad(normed_two, hidden_grad)
    grad_b_up = column_sum(hidden_grad)
    mlp_input_grad, grad_norm2_gain, grad_norm2_shift = norm2_back(project_back(hidden_grad, w_up))
    resid_grad = out_grad + mlp_input_grad
    branch_grad = resid_grad.astype(jnp.bfloat16)
    grad_w_out = weight_grad(attended, branch_grad)
    grad_b_out = column_sum(branch_grad)
    attended_grad = (
        project_back(branch_grad, w_out)
        .astype(jnp.bfloat16)
        .reshape(row_count, local_len, model_width)
    )
    attended_groups = to_groups(attended_grad, row_count, local_len, group_count)

    def backward_pair(items):
        query_pair, key_pair, value_pair, grad_pair, row_top, row_total = items
        probs, prob_grad = probs_and_grads(
            query_pair, key_pair, value_pair, grad_pair, same_image, row_top, row_total, score_scale
        )
        probs_low = probs.astype(jnp.bfloat16)
        score_grad = probs * (prob_grad - jnp.sum(probs * prob_grad, axis=-1, keepdims=True))
        score_low = (score_grad * score_scale).astype(jnp.bfloat16)
        query_part = jnp.einsum(
            "rhqk,rkhe->rqhe", score_low, split_heads(key_pair), preferred_element_type=jnp.float32
        )
        key_part = jnp.einsum(
            "rhqk,rqhe->rkhe",
            score_low,
            split_heads(query_pair),
            preferred_element_type=jnp.float32,
        )
        value_part = jnp.einsum(
            "rhqk,rqhe->rkhe", probs_low, split_heads(grad_pair), preferred_element_type=jnp.float32
        )
        return (
            query_part.astype(jnp.bfloat16).reshape(query_pair.shape),
            key_part.reshape(key_pair.shape),
            value_part.reshape(key_pair.shape),
        )

    query_grad_groups, key_part_groups, value_part_groups = lax.map(
        backward_pair,
        (query_groups, key_groups, value_groups, attended_groups, top_groups, total_groups),
    )
    key_sum, value_sum = (
        lax.psum_scatter(
            from_groups(key_part_groups).astype(jnp.bfloat16),
            "seq",
            scatter_dimension=1,
            tiled=True,
        ).astype(jnp.float32),
        lax.psum_scatter(
            from_groups(value_part_groups).astype(jnp.bfloat16),
            "seq",
            scatter_dimension=1,
            tiled=True,
        ).astype(jnp.float32),
    )
    query_grad = from_groups(query_grad_groups).reshape(token_count, model_width)
    key_grad = key_sum.astype(jnp.bfloat16).reshape(token_count, model_width)
    value_grad = value_sum.astype(jnp.bfloat16).reshape(token_count, model_width)
    grad_w_query = weight_grad(normed, query_grad)
    grad_b_query = column_sum(query_grad)
    grad_w_key = weight_grad(normed, key_grad)
    grad_w_value = weight_grad(normed, value_grad)
    grad_b_value = column_sum(value_grad)
    norm_grad = (
        project_back(query_grad, w_query)
        + project_back(key_grad, w_key)
        + project_back(value_grad, w_value)
    )
    first_input_grad, grad_norm1_gain, grad_norm1_shift = norm1_back(norm_grad)
    grad_tokens = (
        (resid_grad + first_input_grad)
        .astype(jnp.bfloat16)
        .reshape(row_count, local_len, model_width)
    )
    summed = (
        lax.psum_scatter(grad_norm1_gain, ("rows", "seq"), scatter_dimension=0, tiled=True),
        lax.psum_scatter(grad_norm1_shift, ("rows", "seq"), scatter_dimension=0, tiled=True),
        lax.psum_scatter(grad_w_query, ("rows", "seq"), scatter_dimension=0, tiled=True),
        lax.psum_scatter(grad_b_query, ("rows", "seq"), scatter_dimension=0, tiled=True),
        lax.psum_scatter(grad_w_key, ("rows", "seq"), scatter_dimension=0, tiled=True),
        lax.psum_scatter(grad_w_value, ("rows", "seq"), scatter_dimension=0, tiled=True),
        lax.psum_scatter(grad_b_value, ("rows", "seq"), scatter_dimension=0, tiled=True),
        lax.psum_scatter(grad_w_out, ("rows", "seq"), scatter_dimension=0, tiled=True),
        lax.psum_scatter(grad_b_out, ("rows", "seq"), scatter_dimension=0, tiled=True),
        lax.psum_scatter(grad_norm2_gain, ("rows", "seq"), scatter_dimension=0, tiled=True),
        lax.psum_scatter(grad_norm2_shift, ("rows", "seq"), scatter_dimension=0, tiled=True),
        lax.psum_scatter(grad_w_up, ("rows", "seq"), scatter_dimension=0, tiled=True),
        lax.psum_scatter(grad_b_up, ("rows", "seq"), scatter_dimension=0, tiled=True),
        lax.psum_scatter(grad_w_down, ("rows", "seq"), scatter_dimension=0, tiled=True),
        lax.psum_scatter(grad_b_down, ("rows", "seq"), scatter_dimension=0, tiled=True),
    )
    return (
        block_out.astype(jnp.bfloat16).reshape(row_count, local_len, model_width),
        grad_tokens,
        summed[0],
        summed[1],
        summed[2],
        summed[3],
        summed[4],
        summed[5],
        summed[6],
        summed[7],
        summed[8],
        summed[9],
        summed[10],
        summed[11],
        summed[12],
        summed[13],
        summed[14],
    )


def solution(mesh):
    placed = (
        P("rows", "seq", None),
        P("rows", None),
        P("rows", "seq", None),
        P(),
        P(),
        P(),
        P(),
        P(),
        P(),
        P(),
        P(),
        P(),
        P(),
        P(),
        P(),
        P(),
        P(),
        P(),
    )
    return jax.shard_map(
        on_device,
        mesh=mesh,
        in_specs=placed,
        out_specs=(
            P("rows", "seq", None),
            P("rows", "seq", None),
            P(("rows", "seq")),
            P(("rows", "seq")),
            P(("rows", "seq"), None),
            P(("rows", "seq")),
            P(("rows", "seq"), None),
            P(("rows", "seq"), None),
            P(("rows", "seq")),
            P(("rows", "seq"), None),
            P(("rows", "seq")),
            P(("rows", "seq")),
            P(("rows", "seq")),
            P(("rows", "seq"), None),
            P(("rows", "seq")),
            P(("rows", "seq"), None),
            P(("rows", "seq")),
        ),
        check_vma=False,
    )
```

profile of v0, /device:TPU:0, one launch (start us, length us, event | category | flops | bytes accessed | tf_op | source)
XLA Modules:
  0.0 1835.9 jit_solution(1478517190634231269)
XLA Ops:
  21.5 5.9 convolution_convert_fusion
  31.5 5.2 fusion.55
  47.9 35.7 %all-gather.3.cloned.1.call-done = bf16[4,1024,1024]{1,2,0:T(8,128)(2,1)} async-done(((bf16[4,256,1024]{1,2,0:T(8,128)(2,1)}), bf16[4,1024,1024]{1,2,0:T(8,128)(2,1)}) %all-gather.3.cloned.1.call-update) | async-done | bytes 8388624 | tf_op jit(solution)/shard_map/all_gather | solution.py:132
  83.7 8.3 copy.76
  92.0 52.7 %all-gather.5.cloned.1.call-done = bf16[4,1024,1024]{1,2,0:T(8,128)(2,1)} async-done(((bf16[4,256,1024]{1,2,0:T(8,128)(2,1)}), bf16[4,1024,1024]{1,2,0:T(8,128)(2,1)}) %all-gather.5.cloned.1.call-update) | async-done | bytes 8388624 | tf_op jit(solution)/shard_map/all_gather | solution.py:131
  144.7 8.2 copy.77
  154.4 104.6 %while.30 = (s32[]{:T(128)}, bf16[8,4,256,128]{2,3,1,0:T(8,128)(2,1)}, f32[8,4,2,256,1]{3,2,1,4,0:T(2,128)}, f32[8,4,2,256,1]{3,2,1,4,0:T(2,128)}, bf16[8,4,1024...) while((s32[]{:T(128)}, ...), condition=%wide.region_5.6_spmd.clone, body=%wide.region_2.5_spmd.clone.sunk | while | flops 563212288 | bytes 37318784 | solution.py:155
  263.3 5.4 fusion.82
  270.0 11.9 fusion.77
  281.9 55.4 %convert_reduce_fusion = (f32[4096]{0:T(1024)}, bf16[1024,4096]{1,0:T(8,128)(2,1)}, f32[1024,4096]{1,0:T(8,128)}) fusion(f32[1024,4096]{1,0:T(8,128)S(1)} %fusion.77, f32[4096]{0:T(1024)S(1)} %copy-done.41, bf16[1024,1024]{1,0:T(8,128)(2,1)} %fusion.53, bf16[4096,1024]{1,0:T(8,128)(2,1)} %param.38), kind=kOutput, calls=%fused_computation.46 | convolution fusion | flops 8904503296 | bytes 52461568 | tf_op jit(solution)/shard_map/dot_general | solution.py:29
  337.3 16.3 multiply_reduce_fusion.1
  368.9 380.9 %while.31 = (s32[]{:T(128)}, bf16[8,4,256,128]{2,3,1,0:T(8,128)(2,1)}, bf16[8,4,1024,128]{2,3,0,1:T(8,128)(2,1)}, bf16[8,4,1024,128]{2,3,0,1:T(8,128)(2,1)}, bf1...) while((s32[]{:T(128)}, ...), condition=%wide.region_12.13_spmd.clone, body=%wide.region_10.12_spmd.clone.sunk | while | flops 1374820352 | bytes 78450864 | solution.py:211
  383.0 13.4 fusion.163
  398.0 12.4 fusion.164
  430.6 13.3 fusion.163
  445.6 12.4 fusion.164
  478.1 13.4 fusion.163
  493.1 12.4 fusion.164
  516.1 5.0 exponential_divide_fusion.2
  525.7 13.4 fusion.163
  540.7 12.4 fusion.164
  563.7 5.0 exponential_divide_fusion.2
  573.2 13.3 fusion.163
  588.3 12.4 fusion.164
  611.3 5.0 exponential_divide_fusion.2
  620.8 13.4 fusion.163
  635.9 12.4 fusion.164
  668.4 13.4 fusion.163
  683.4 12.4 fusion.164
  716.0 13.4 fusion.163
  731.0 12.4 fusion.164
  758.8 7.6 fusion.56
  766.6 6.6 fusion.60
  773.3 48.4 %reduce-scatter.9.cloned.1.call-done = bf16[4,256,1024]{1,2,0:T(8,128)(2,1)} async-done(((bf16[4,1024,1024]{1,2,0:T(8,128)(2,1)}), bf16[4,256,1024]{1,2,0:T(8,128)(2,1)}) %reduce-scatter.9.cloned.1.call-update) | async-done | bytes 2097168 | tf_op jit(solution)/shard_map/reduce_scatter | solution.py:216
  821.7 6.5 convolution_bitcast_fusion.1
  828.3 67.8 %reduce-scatter.11.cloned.1.call-done = bf16[4,256,1024]{1,2,0:T(8,128)(2,1)} async-done(((bf16[4,1024,1024]{1,2,0:T(8,128)(2,1)}), bf16[4,256,1024]{1,2,0:T(8,128)(2,1)}) %reduce-scatter.11.cloned.1.call-update) | async-done | bytes 2097168 | tf_op jit(solution)/shard_map/reduce_scatter | solution.py:222
  896.1 6.6 convolution_bitcast_fusion
  903.4 16.8 fusion.76
  920.9 12.4 multiply_convert_fusion.1
  936.6 11.5 fusion.85
  957.7 12.2 add_convert_fusion.2
  990.6 40.7 %all-reduce.9 = (f32[1024]{0:T(1024)S(1)}, f32[1024]{0:T(1024)S(1)}, f32[1024]{0:T(1024)S(1)}, f32[1024]{0:T(1024)S(1)}, f32[1024]{0:T(1024)S(1)}, /*index=5*/f3...) all-reduce(f32[1024]{0:T(1024)S(1)} %get-tuple-element.241, ...), channel_id=4, replica_groups=mesh['rows'=8,'seq'=4] {'rows','seq'}, use_global_device_ids=true, to_apply=%region_18.19.clone | all-reduce | flops 12288 | bytes 98304
  1036.6 6.8 add_convert_fusion.1
  1043.4 136.7 %reduce-scatter.19.cloned.1.call-done = f32[32,1024]{1,0:T(8,128)} async-done(((f32[1024,1024]{1,0:T(8,128)}), f32[32,1024]{1,0:T(8,128)}) %reduce-scatter.19.cloned.1.call-update) | async-done | bytes 131088 | tf_op jit(solution)/shard_map/reduce_scatter | solution.py:256
  1180.1 139.7 %reduce-scatter.15.cloned.1.call-done = f32[32,1024]{1,0:T(8,128)} async-done(((f32[1024,1024]{1,0:T(8,128)}), f32[32,1024]{1,0:T(8,128)}) %reduce-scatter.15.cloned.1.call-update) | async-done | bytes 131088 | tf_op jit(solution)/shard_map/reduce_scatter | solution.py:253
  1319.8 139.7 %reduce-scatter.17.cloned.1.call-done = f32[32,1024]{1,0:T(8,128)} async-done(((f32[1024,1024]{1,0:T(8,128)}), f32[32,1024]{1,0:T(8,128)}) %reduce-scatter.17.cloned.1.call-update) | async-done | bytes 131088 | tf_op jit(solution)/shard_map/reduce_scatter | solution.py:254
  1459.5 181.8 %reduce-scatter.21.cloned.1.call-done = f32[32,4096]{1,0:T(8,128)} async-done(((f32[1024,4096]{1,0:T(8,128)}), f32[32,4096]{1,0:T(8,128)}) %reduce-scatter.21.cloned.1.call-update) | async-done | bytes 524304 | tf_op jit(solution)/shard_map/reduce_scatter | solution.py:260
  1641.3 187.3 %reduce-scatter.23.cloned.1.call-done = f32[128,1024]{1,0:T(8,128)} async-done(((f32[4096,1024]{1,0:T(8,128)}), f32[128,1024]{1,0:T(8,128)}) %reduce-scatter.23.cloned.1.call-update) | async-done | bytes 524304 | tf_op jit(solution)/shard_map/reduce_scatter | solution.py:262
  (377 shorter events, 363.9 us)
Async XLA Ops:
  7.2 6.6 copy-start
  7.2 5.7 copy-start.50
  7.2 5.7 copy-start.28
  7.2 6.5 copy-start.59
  7.2 76.4 %all-gather.3.cloned.1.call-start = ((), (), s32[]{:S(2)}) async-start(), calls=%async_computation.8 | async-start | bytes 10485760 | tf_op jit(solution)/shard_map/all_gather | solution.py:132
  7.3 5.6 copy-start.1
  12.3 5.1 copy-start.24
  12.9 4.6 copy-start.26
  21.4 123.2 %all-gather.5.cloned.1.call-start = ((), (), s32[]{:S(2)}) async-start(), calls=%async_computation.9 | async-start | bytes 10485760 | tf_op jit(solution)/shard_map/all_gather | solution.py:131
  31.4 790.3 %reduce-scatter.9.cloned.1.call-start = ((), (), s32[]{:S(2)}) async-start(), calls=%async_computation.10 | async-start | bytes 10485760 | tf_op jit(solution)/shard_map/reduce_scatter | solution.py:216
  36.7 6.7 copy-start.17
  268.7 13.1 copy-start.6
  268.8 13.1 copy-start.36
  270.0 11.9 copy-start.45
  270.0 11.9 copy-start.41
  281.9 55.4 %copy-start.5 = (f32[1024,4096]{1,0:T(8,128)}, f32[1024,4096]{1,0:T(8,128)S(1)}, u32[]{:S(2)}) copy-start(f32[1024,4096]{1,0:T(8,128)S(1)} %fusion.77) | copy-start | bytes 50331652
  281.9 55.4 %copy-start.53 = (f32[1024]{0:T(1024)S(1)}, f32[1024]{0:T(1024)}, u32[]{:S(2)}) copy-start(f32[1024]{0:T(1024)} %param.34) | copy-start | bytes 12292
  337.3 16.3 copy-start.40
  337.3 16.3 copy-start.7
  337.3 16.3 copy-start.37
  337.3 16.3 copy-start.46
  362.9 5.9 copy-start.18
  362.9 5.9 copy-start.20
  373.5 5.0 copy-start.12
  421.0 5.0 copy-start.12
  468.6 5.0 copy-start.12
  516.1 5.0 copy-start.12
  563.7 5.0 copy-start.12
  611.3 5.0 copy-start.12
  658.8 5.0 copy-start.12
  706.4 5.0 copy-start.12
  749.8 146.3 %reduce-scatter.11.cloned.1.call-start = ((), (), s32[]{:S(2)}) async-start(), calls=%async_computation.11 | async-start | bytes 10485760 | tf_op jit(solution)/shard_map/reduce_scatter | solution.py:222
  750.4 293.0 %reduce-scatter.13.cloned.1.call-start = ((), (), s32[]{:S(2)}) async-start(), calls=%async_computation.12 | async-start | bytes 4325376 | tf_op jit(solution)/shard_map/reduce_scatter | solution.py:251
  766.4 413.7 %reduce-scatter.19.cloned.1.call-start = ((), (), s32[]{:S(2)}) async-start(), calls=%async_computation.15 | async-start | bytes 4325376 | tf_op jit(solution)/shard_map/reduce_scatter | solution.py:256
  773.2 546.6 %reduce-scatter.15.cloned.1.call-start = ((), (), s32[]{:S(2)}) async-start(), calls=%async_computation.13 | async-start | bytes 4325376 | tf_op jit(solution)/shard_map/reduce_scatter | solution.py:253
  828.2 631.3 %reduce-scatter.17.cloned.1.call-start = ((), (), s32[]{:S(2)}) async-start(), calls=%async_computation.14 | async-start | bytes 4325376 | tf_op jit(solution)/shard_map/reduce_scatter | solution.py:254
  902.7 738.7 %reduce-scatter.21.cloned.1.call-start = ((), (), s32[]{:S(2)}) async-start(), calls=%async_computation.16 | async-start | bytes 17301504 | tf_op jit(solution)/shard_map/reduce_scatter | solution.py:260
  920.2 908.4 %reduce-scatter.23.cloned.1.call-start = ((), (), s32[]{:S(2)}) async-start(), calls=%async_computation.17 | async-start | bytes 17301504 | tf_op jit(solution)/shard_map/reduce_scatter | solution.py:262
  920.9 15.7 copy-start.13
  948.1 5.1 copy-start.14
  948.1 5.1 copy-start.58
  951.2 6.5 slice-start
  980.1 4.8 copy-start.2
  980.1 4.8 copy-start.16
  980.1 4.8 copy-start.27
  980.1 4.8 copy-start.65
  988.1 48.5 %copy-start.23 = (f32[1,2,4,128]{3,1,2,0:T(2,128)S(1)}, f32[1,2,4,128]{3,1,2,0:T(2,128)}, u32[]{:S(2)}) copy-start(f32[1,2,4,128]{3,1,2,0:T(2,128)} %copy-done.21) | copy-start | bytes 12292
  988.1 48.5 %copy-start.31 = (f32[1024]{0:T(1024)S(1)}, f32[1024]{0:T(1024)}, u32[]{:S(2)}) copy-start(f32[1024]{0:T(1024)} %copy-done.30) | copy-start | bytes 12292
  (37 other events, 80.2 us)
Sparse Core Ops, SparseCore 0:
  21.5 62.0 all-gather.2
  85.2 59.3 all-gather.4
  749.9 71.7 reduce-scatter.8
  824.3 71.7 reduce-scatter.10
  898.7 141.3 reduce-scatter.12
  1042.8 137.2 reduce-scatter.18
  1183.0 136.8 reduce-scatter.14
  1322.7 136.8 reduce-scatter.16
  1462.4 178.8 reduce-scatter.20
  1644.1 184.5 reduce-scatter.22
where the time goes:
time: 1850 us; the launch traced here: 1840 us
  waiting for transfers between devices  990 us (54%)
  matrix products  543 us (29%)
  local copies, waits for them, and re-layouts  169 us (9%)
  other arithmetic  75.4 us (4%)
  blocking collectives  40.7 us (2%)
    reduce_scatter x1, waiting for transfers between devices, on_device(): lax.psum_scatter(grad_w_down, ('rows', 'seq'), scatter_dimension=0, tiled...  187 us
    reduce_scatter x1, waiting for transfers between devices, on_device(): lax.psum_scatter(grad_w_up, ('rows', 'seq'), scatter_dimension=0, tiled=T...  182 us
    reduce_scatter x1, waiting for transfers between devices, on_device(): lax.psum_scatter(grad_w_key, ('rows', 'seq'), scatter_dimension=0, tiled=...  140 us
    reduce_scatter x1, waiting for transfers between devices, on_device(): lax.psum_scatter(grad_w_value, ('rows', 'seq'), scatter_dimension=0, tile...  140 us
    reduce_scatter x1, waiting for transfers between devices, on_device(): lax.psum_scatter(grad_w_out, ('rows', 'seq'), scatter_dimension=0, tiled=...  137 us
    dot_general x8, matrix products, backward_pair(): jnp.einsum('rhqk,rkhe->rqhe', score_low, split_heads(key_pair), preferred...  107 us
    dot_general x8, matrix products, backward_pair(): jnp.einsum('rhqk,rqhe->rkhe', score_low, split_heads(query_pair), preferr...  99.5 us
    dot_general x6, matrix products, project_back(): lax.dot_general(left_side, matrix, (((1,), (1,)), ((), ())), preferred_el...  86.2 us
  transfers between devices with their start and end apart: 10, of which 9 were waited for; matrix products, arithmetic and copies ran while one was open for 9% of the time, Pallas kernels for 0%

commit v1 on v0

v1 whole, which is shorter than its diff:
```python
import jax
import jax.numpy as jnp
import numpy as np
from jax import lax
from jax.experimental import pallas as pl
from jax.experimental.pallas import tpu as pltpu
from jax.sharding import PartitionSpec as P

HEADS = 16
norm_eps = 1e-06
bf16 = jnp.bfloat16
f32 = jnp.float32
MIB = 1024 * 1024
DIGITS, BASE = 3, 11
CODE = DIGITS * BASE
HALF = 64


def dg(a, b, ca, cb):
    return lax.dot_general(a, b, (((ca,), (cb,)), ((), ())), preferred_element_type=f32)


def params(mib):
    return pltpu.CompilerParams(vmem_limit_bytes=mib * MIB)


def cost(flops, bytes_accessed, transcendentals=0):
    return pl.CostEstimate(
        flops=flops, bytes_accessed=bytes_accessed, transcendentals=transcendentals
    )


def norm_parts(values):
    mean = jnp.mean(values, axis=-1, keepdims=True)
    centered = values - mean
    variance = jnp.mean(centered * centered, axis=-1, keepdims=True)
    rstd = lax.rsqrt(variance + norm_eps)
    return centered * rstd, rstd


def qkv_kernel(first, c0, c1, gain, shift, wq, wk, wv, bq, bv, *refs):
    x, normed, qT, k, kT, v, vT, n_scr = refs[-8:]
    step = pl.program_id(0)
    length = c0.shape[0]

    @pl.when(step == 0)
    def _():
        for j, chunk in enumerate((c0, c1)):
            rows = slice(j * length, (j + 1) * length)
            values = chunk[...]
            x[rows, :] = values
            n, _ = norm_parts(values.astype(f32))
            low = (n * gain[...] + shift[...]).astype(bf16)
            n_scr[rows, :] = low
            normed[rows, :] = low

    n = n_scr[...]
    q_new = (dg(n, wq[...], 1, 0) + bq[...]).astype(bf16)
    qT[...] = (q_new.astype(f32) * 0.125).astype(bf16).T
    k_new = dg(n, wk[...], 1, 0).astype(bf16)
    k[...] = k_new
    kT[...] = k_new.T
    v_new = (dg(n, wv[...], 1, 0) + bv[...]).astype(bf16)
    v[...] = v_new
    vT[...] = v_new.T


def qkv(half, chunks, gain, shift, wq, wk, wv, bq, bv, before):
    length, width = chunks[0].shape
    total = 4 * length
    block = 256
    steps = width // block
    vec = pl.BlockSpec((1, width), lambda i: (0, 0))
    whole = pl.BlockSpec((length, width), lambda i: (0, 0))
    part = pl.BlockSpec((width, block), lambda i: (0, i))
    bias = pl.BlockSpec((1, block), lambda i: (0, i))
    wide = pl.BlockSpec((2 * length, width), lambda i: (half, 0))
    rows = pl.BlockSpec((2 * length, block), lambda i: (half, i))
    cols = pl.BlockSpec((block, 2 * length), lambda i: (i, half))
    out = jax.ShapeDtypeStruct((total, width), bf16)
    outT = jax.ShapeDtypeStruct((width, total), bf16)
    anyspec = pl.BlockSpec(memory_space=pl.ANY)
    return pl.pallas_call(
        lambda *refs: qkv_kernel(half == 0, *refs),
        grid=(steps,),
        in_specs=[whole, whole, vec, vec, part, part, part, bias, bias] + [anyspec] * len(before),
        out_specs=[wide, wide, cols, rows, cols, rows, cols],
        out_shape=[out, out, outT, out, outT, out, outT],
        scratch_shapes=[pltpu.VMEM((2 * length, width), bf16)],
        input_output_aliases={9 + n: n for n in range(len(before))},
        compiler_params=params(40),
        cost_estimate=cost(2 * 2 * length * width * 3 * width, 20 * MIB),
    )(chunks[0], chunks[1], gain, shift, wq, wk, wv, bq, bv, *before)


def attend_kernel(qT, k, vT, fT, g, oT, olo, aux):
    total = k.shape[0]
    lane = lax.broadcasted_iota(jnp.int32, (total, 128), 1)
    row = lax.broadcasted_iota(jnp.int32, (HALF, total), 0)
    keys, codes, queries_code = k[...], g[...], fT[...]
    ones = jnp.ones((16, total), bf16)

    def score(h):
        ka = jnp.where((lane < HALF) == (h == 0), keys, codes)
        qh = qT[h * HALF : (h + 1) * HALF, :]
        qa = jnp.concatenate([qh, queries_code] if h == 0 else [queries_code, qh], 0)
        s = dg(ka, qa, 1, 0)
        return s, jnp.max(s, axis=0, keepdims=True)

    def finish(h, s, top):
        head = slice(h * HALF, (h + 1) * HALF)
        va = jnp.concatenate([vT[head, :], ones], 0)
        p = jnp.exp(s - top).astype(bf16)
        mixed = dg(va, p, 1, 0)
        weight = mixed[HALF : HALF + 1]
        out = mixed[:HALF] / weight
        low = out.astype(bf16)
        oT[head, :] = low
        olo[head, :] = (out - low.astype(f32)).astype(bf16)
        aux[head, :] = pieces(
            -(top + jnp.log(weight)), row, queries_code.astype(f32)
        ).astype(bf16)

    first = score(0)
    second = score(1)
    finish(0, *first)
    finish(1, *second)


def pieces(value, row, base):
    hi = value.astype(bf16).astype(f32)
    mid = (value - hi).astype(bf16).astype(f32)
    low = value - hi - mid
    return jnp.where(
        row == CODE, hi, jnp.where(row == CODE + 1, mid, jnp.where(row == CODE + 2, low, base))
    )


def attend(qT, k, vT, fT, g):
    width, total = qT.shape
    pair = pl.BlockSpec((128, total), lambda i: (i, 0))
    return pl.pallas_call(
        attend_kernel,
        grid=(width // 128,),
        in_specs=[
            pair,
            pl.BlockSpec((total, 128), lambda i: (0, i)),
            pair,
            pl.BlockSpec((HALF, total), lambda i: (0, 0)),
            pl.BlockSpec((total, 128), lambda i: (0, 0)),
        ],
        out_specs=[pair] * 3,
        out_shape=[jax.ShapeDtypeStruct((width, total), bf16)] * 3,
        compiler_params=params(56),
        cost_estimate=cost(16 * HEADS * total * total * 64, 12 * MIB, HEADS * total * total),
    )(qT, k, vT, fT, g)


def attend_back_kernel(qT, k, kT, v, doT, oT, olo, aux, g, dqT, dkT, dvT):
    total = k.shape[0]
    lane = lax.broadcasted_iota(jnp.int32, (total, 128), 1)
    row = lax.broadcasted_iota(jnp.int32, (HALF, total), 0)
    keys, values, codes = k[...], v[...], g[...]
    for h in range(2):
        head = slice(h * HALF, (h + 1) * HALF)
        mine = (lane < HALF) == (h == 0)
        ka = jnp.where(mine, keys, codes)
        va = jnp.where(mine, values, codes)
        doh, qh, ax = doT[head, :], qT[head, :], aux[head, :]
        full = oT[head, :].astype(f32) + olo[head, :].astype(f32)
        delta = -jnp.sum(doh.astype(f32) * full, axis=0, keepdims=True)
        dx = pieces(delta, row, 0.0).astype(bf16)
        qa = jnp.concatenate([qh, ax] if h == 0 else [ax, qh], 0)
        doa = jnp.concatenate([doh, dx] if h == 0 else [dx, doh], 0)
        s = dg(ka, qa, 1, 0)
        dp = dg(va, doa, 1, 0)
        p = jnp.exp(s)
        low = p.astype(bf16)
        ds = (p * dp).astype(bf16)
        dkT[head, :] = dg(qh, ds, 1, 1).astype(bf16)
        dvT[head, :] = dg(doh, low, 1, 1).astype(bf16)
        dqT[head, :] = (dg(kT[head, :], ds, 1, 0) * 0.125).astype(bf16)


def attend_back(qT, k, kT, v, doT, oT, olo, aux, g):
    width, total = qT.shape
    pair = pl.BlockSpec((128, total), lambda i: (i, 0))
    tall = pl.BlockSpec((total, 128), lambda i: (0, i))
    return pl.pallas_call(
        attend_back_kernel,
        grid=(width // 128,),
        in_specs=[pair, tall, pair, tall, pair, pair, pair, pair]
        + [pl.BlockSpec((total, 128), lambda i: (0, 0))],
        out_specs=[pair] * 3,
        out_shape=[jax.ShapeDtypeStruct((width, total), bf16)] * 3,
        compiler_params=params(56),
        cost_estimate=cost(40 * HEADS * total * total * 64, 22 * MIB, HEADS * total * total),
    )(qT, k, kT, v, doT, oT, olo, aux, g)


def out_kernel(oT, x, w, b, gain, shift, residual, normed):
    r = x[...].astype(f32) + dg(oT[...], w[...], 0, 0) + b[...]
    residual[...] = r
    n, _ = norm_parts(r)
    normed[...] = (n * gain[...] + shift[...]).astype(bf16)


def out_project(oT, x, w, b, gain, shift):
    total, width = x.shape
    block = 256
    vec = pl.BlockSpec((1, width), lambda i: (0, 0))
    rows = pl.BlockSpec((block, width), lambda i: (i, 0))
    return pl.pallas_call(
        out_kernel,
        grid=(total // block,),
        in_specs=[
            pl.BlockSpec((width, block), lambda i: (0, i)),
            rows,
            pl.BlockSpec((width, width), lambda i: (0, 0)),
            vec,
            vec,
            vec,
        ],
        out_specs=[rows, rows],
        out_shape=[
            jax.ShapeDtypeStruct((total, width), f32),
            jax.ShapeDtypeStruct((total, width), bf16),
        ],
        compiler_params=params(40),
        cost_estimate=cost(2 * total * width * width, 12 * MIB),
    )(oT, x, w, b, gain, shift)


def mlp_kernel(n2, di, wu, wd, bu, res, bd, out, dn, gwd, gwu, gbu, acc_o, acc_n):
    step = pl.program_id(0)

    @pl.when(step == 0)
    def _():
        acc_o[...] = jnp.zeros_like(acc_o)
        acc_n[...] = jnp.zeros_like(acc_n)

    pre = dg(n2[...], wu[...], 1, 0) + bu[...]
    dact = dg(di[...], wd[...], 1, 1)
    cdf = 0.5 * (1.0 + lax.erf(pre * np.float32(np.sqrt(0.5))))
    pdf = jnp.exp(-0.5 * pre * pre) * np.float32(1 / np.sqrt(2 * np.pi))
    act = (pre * cdf).astype(bf16)
    hidden = (dact * (cdf + pre * pdf)).astype(bf16)
    acc_o[...] += dg(act, wd[...], 1, 0)
    acc_n[...] += dg(hidden, wu[...], 1, 1)
    gwd[...] = dg(act, di[...], 0, 0).astype(bf16)
    gwu[...] = dg(n2[...], hidden, 0, 0).astype(bf16)
    gbu[...] = jnp.sum(hidden.astype(f32), axis=0, keepdims=True)

    @pl.when(step == pl.num_programs(0) - 1)
    def _():
        out[...] = (res[...] + acc_o[...] + bd[...]).astype(bf16)
        dn[...] = acc_n[...]


def mlp(n2, di, wu, wd, bu, res, bd):
    total, width = n2.shape
    hidden = wu.shape[1]
    block = 512

    def full():
        return pl.BlockSpec((total, width), lambda i: (0, 0), pipeline_mode=pl.Buffered(1))

    up = pl.BlockSpec((width, block), lambda i: (0, i))
    down = pl.BlockSpec((block, width), lambda i: (i, 0))
    bias = pl.BlockSpec((1, block), lambda i: (0, i))
    return pl.pallas_call(
        mlp_kernel,
        grid=(hidden // block,),
        in_specs=[full(), full(), up, down, bias, full()]
        + [pl.BlockSpec((1, width), lambda i: (0, 0))],
        out_specs=[full(), full(), down, up, bias],
        out_shape=[
            jax.ShapeDtypeStruct((total, width), bf16),
            jax.ShapeDtypeStruct((total, width), f32),
            jax.ShapeDtypeStruct((hidden, width), bf16),
            jax.ShapeDtypeStruct((width, hidden), bf16),
            jax.ShapeDtypeStruct((1, hidden), f32),
        ],
        scratch_shapes=[pltpu.VMEM((total, width), f32)] * 2,
        compiler_params=params(56),
        cost_estimate=cost(12 * total * width * hidden, 50 * MIB, 2 * total * hidden),
    )(n2, di, wu, wd, bu, res, bd)


def out_back_kernel(dn, res, di, oT, w, gain, doT, rg, gw, ggain, gshift, gb, acc):
    step = pl.program_id(0)

    @pl.when(step == 0)
    def _():
        acc[...] = jnp.zeros_like(acc)
        ggain[...] = jnp.zeros_like(ggain)
        gshift[...] = jnp.zeros_like(gshift)
        gb[...] = jnp.zeros_like(gb)

    n, rstd = norm_parts(res[...])
    grad = dn[...]
    ggain[...] += jnp.sum(grad * n, axis=0, keepdims=True)
    gshift[...] += jnp.sum(grad, axis=0, keepdims=True)
    gh = grad * gain[...]
    mean = jnp.mean(gh, axis=-1, keepdims=True)
    tilt = jnp.mean(gh * n, axis=-1, keepdims=True)
    resid = di[...].astype(f32) + rstd * (gh - mean - n * tilt)
    rg[...] = resid
    low = resid.astype(bf16)
    gb[...] += jnp.sum(low.astype(f32), axis=0, keepdims=True)
    doT[...] = dg(w[...], low, 1, 1).astype(bf16)
    acc[...] += dg(oT[...], low, 1, 0)

    @pl.when(step == pl.num_programs(0) - 1)
    def _():
        gw[...] = acc[...].astype(bf16)


def out_back(dn, res, di, oT, w, gain):
    total, width = res.shape
    block = 256
    vec = pl.BlockSpec((1, width), lambda i: (0, 0))
    rows = pl.BlockSpec((block, width), lambda i: (i, 0))
    cols = pl.BlockSpec((width, block), lambda i: (0, i))
    square = pl.BlockSpec((width, width), lambda i: (0, 0))
    row = jax.ShapeDtypeStruct((1, width), f32)
    return pl.pallas_call(
        out_back_kernel,
        grid=(total // block,),
        in_specs=[rows, rows, rows, cols, square, vec],
        out_specs=[cols, rows, square, vec, vec, vec],
        out_shape=[
            jax.ShapeDtypeStruct((width, total), bf16),
            jax.ShapeDtypeStruct((total, width), f32),
            jax.ShapeDtypeStruct((width, width), bf16),
            row,
            row,
            row,
        ],
        scratch_shapes=[pltpu.VMEM((width, width), f32)],
        compiler_params=params(40),
        cost_estimate=cost(4 * total * width * width, 24 * MIB),
    )(dn, res, di, oT, w, gain)


def qkv_grad_kernel(n, dqT, dkT, dvT, gq, gk, gv, bq, bv):
    total = n.shape[0]
    ones = jnp.ones((8, total), bf16)
    gq[...] = dg(n[...], dqT[...], 0, 1).astype(bf16)
    gk[...] = dg(n[...], dkT[...], 0, 1).astype(bf16)
    gv[...] = dg(n[...], dvT[...], 0, 1).astype(bf16)
    bq[...] = dg(ones, dqT[...], 1, 1)[:1]
    bv[...] = dg(ones, dvT[...], 1, 1)[:1]


def qkv_grad(n, dqT, dkT, dvT):
    total, width = n.shape
    block = 256
    rows = pl.BlockSpec((block, total), lambda i: (i, 0))
    cols = pl.BlockSpec((width, block), lambda i: (0, i))
    bias = pl.BlockSpec((1, block), lambda i: (0, i))
    square = jax.ShapeDtypeStruct((width, width), bf16)
    row = jax.ShapeDtypeStruct((1, width), f32)
    return pl.pallas_call(
        qkv_grad_kernel,
        grid=(width // block,),
        in_specs=[pl.BlockSpec((total, width), lambda i: (0, 0)), rows, rows, rows],
        out_specs=[cols, cols, cols, bias, bias],
        out_shape=[square, square, square, row, row],
        compiler_params=params(40),
        cost_estimate=cost(6 * total * width * width, 14 * MIB),
    )(n, dqT, dkT, dvT)


def token_grad_kernel(dqT, dkT, dvT, wq, wk, wv, x, rg, gain, out, ggain, gshift, acc):
    step = pl.program_id(0)
    new = dg(dqT[...], wq[...], 0, 1) + dg(dkT[...], wk[...], 0, 1) + dg(dvT[...], wv[...], 0, 1)

    @pl.when(step == 0)
    def _():
        acc[...] = new

    @pl.when(step > 0)
    def _():
        acc[...] += new

    @pl.when(step == pl.num_programs(0) - 1)
    def _():
        n, rstd = norm_parts(x[...].astype(f32))
        grad = acc[...]
        ggain[...] = jnp.sum(grad * n, axis=0, keepdims=True)
        gshift[...] = jnp.sum(grad, axis=0, keepdims=True)
        gh = grad * gain[...]
        mean = jnp.mean(gh, axis=-1, keepdims=True)
        tilt = jnp.mean(gh * n, axis=-1, keepdims=True)
        out[...] = (rg[...] + rstd * (gh - mean - n * tilt)).astype(bf16)


def token_grad(half, dqT, dkT, dvT, wq, wk, wv, x, rg, gain):
    total, width = x.shape
    block = 256
    part = pl.BlockSpec((block, total // 2), lambda i: (i, half))
    weight = pl.BlockSpec((width, block), lambda i: (0, i))
    wide = pl.BlockSpec((total // 2, width), lambda i: (half, 0))
    vec = pl.BlockSpec((1, width), lambda i: (0, 0))
    row = jax.ShapeDtypeStruct((1, width), f32)
    return pl.pallas_call(
        token_grad_kernel,
        grid=(width // block,),
        in_specs=[part, part, part, weight, weight, weight, wide, wide, vec],
        out_specs=[pl.BlockSpec((total // 2, width), lambda i: (0, 0)), vec, vec],
        out_shape=[jax.ShapeDtypeStruct((total // 2, width), bf16), row, row],
        scratch_shapes=[pltpu.VMEM((total // 2, width), f32)],
        compiler_params=params(40),
        cost_estimate=cost(3 * total * width * width, 14 * MIB),
    )(dqT, dkT, dvT, wq, wk, wv, x, rg, gain)


def swap(values, axis, size, bit):
    return lax.ppermute(values, axis, [(i, i ^ bit) for i in range(size)])


def halving(values, order, sizes):
    rows, seq = sizes
    bits = (rows * seq).bit_length() - 1
    seq_bits = seq.bit_length() - 1
    chunk = values.shape[0] // (rows * seq)
    spots = list(range(bits - 1, -1, -1))
    kept = values.reshape((2,) * bits + (chunk,) + values.shape[1:])
    got = None
    for n, bit in enumerate(order):
        at = spots.index(bit)
        spots.remove(bit)
        axis, size, flip = ("seq", seq, 1 << bit) if bit < seq_bits else ("rows", rows, 1 << (bit - seq_bits))
        mine = (lax.axis_index(axis) // flip) % 2

        def half(which):
            own = lax.dynamic_index_in_dim(kept, which, at, keepdims=False)
            if got is None:
                return own
            other = lax.dynamic_index_in_dim(got, which, at, keepdims=False)
            return (own.astype(f32) + other.astype(f32)).astype(values.dtype)

        send, kept = half(1 - mine), half(mine)
        got = swap(send, axis, size, flip)
    return kept.astype(f32) + got.astype(f32)


def on_device(
    tokens,
    segment_ids,
    grad_out,
    norm1_gain,
    norm1_shift,
    w_query,
    b_query,
    w_key,
    w_value,
    b_value,
    w_out,
    b_out,
    norm2_gain,
    norm2_shift,
    w_up,
    b_up,
    w_down,
    b_down,
):
    row_count, local_len, width = tokens.shape
    full_len = segment_ids.shape[1]
    seq = lax.axis_size("seq")
    rows = lax.axis_size("rows")
    sizes = (rows, seq)
    me = lax.axis_index("seq")
    assert row_count == seq == 4 and local_len * seq == full_len

    def vec(v):
        return v.reshape(1, -1)

    def pick(values, j):
        return lax.dynamic_index_in_dim(values, me ^ j, 0, keepdims=False)

    def scatter_rows(values):
        return [pick(values, 0)] + [
            swap(pick(values, j), "seq", seq, j) for j in range(1, seq)
        ]

    def gather_rows(chunks):
        back = [chunks[0]] + [swap(chunks[j], "seq", seq, j) for j in range(1, seq)]
        out = jnp.zeros((row_count, local_len, width), bf16)
        for j in range(seq):
            out = lax.dynamic_update_index_in_dim(out, back[j], me ^ j, 0)
        return out

    ids_rows = lax.dynamic_index_in_dim(segment_ids, me, 0, keepdims=False).reshape(seq, local_len)
    ids = jnp.concatenate([pick(ids_rows, j) for j in range(seq)])
    digits = jnp.stack([(ids // BASE**n) % BASE for n in range(DIGITS)], 1)
    hot = (digits[:, :, None] == jnp.arange(BASE)[None, None, :]).reshape(full_len, CODE)
    hot = hot.astype(f32)
    rest = jnp.zeros((full_len, HALF - CODE), f32)
    query_code = jnp.concatenate([hot, rest], 1).astype(bf16).T
    key_code = jnp.concatenate([-1e30 * (1.0 - hot), rest.at[:, :3].set(1.0)], 1).astype(bf16)
    key_code = jnp.concatenate([key_code, key_code], 1)

    x_chunks = scatter_rows(tokens)
    norm1 = (vec(norm1_gain), vec(norm1_shift))
    weights = (w_query, w_key, w_value, vec(b_query), vec(b_value))
    before = qkv(0, x_chunks[:2], *norm1, *weights, ())
    x, normed, qT, k, kT, v, vT = qkv(1, x_chunks[2:], *norm1, *weights, before)

    local_ids = lax.dynamic_slice_in_dim(segment_ids, me * local_len, local_len, 1)
    is_image = (local_ids != full_len).astype(bf16)[:, :, None]
    out_grad = grad_out * is_image
    down_in = jnp.concatenate(scatter_rows(out_grad), 0)
    grad_b_down = jnp.sum(out_grad.astype(f32), axis=(0, 1))

    oT, olo, aux = attend(qT, k, vT, query_code, key_code)
    residual, normed_two = out_project(
        oT, x, w_out, vec(b_out), vec(norm2_gain), vec(norm2_shift)
    )
    block_out, dn, grad_w_down, grad_w_up, grad_b_up = mlp(
        normed_two, down_in, w_up, w_down, vec(b_up), residual, vec(b_down)
    )
    block_out = gather_rows([block_out[j * local_len : (j + 1) * local_len] for j in range(seq)])

    nbits = (rows * seq).bit_length() - 1
    seq_bits = seq.bit_length() - 1
    high = list(range(seq_bits, nbits))
    x_first = [0] + high[:1] + list(range(1, seq_bits)) + high[1:]
    y_first = [0] + list(range(1, seq_bits)) + high
    z_first = [0] + high[1:] + high[:1] + list(range(1, seq_bits))
    grad_w_down = halving(grad_w_down, x_first, sizes)
    grad_w_up = halving(grad_w_up, z_first, sizes)

    doT, resid_grad, grad_w_out, grad_gain2, grad_shift2, grad_b_out = out_back(
        dn, residual, down_in, oT, w_out, vec(norm2_gain)
    )
    grad_w_out = halving(grad_w_out, y_first, sizes)

    dqT, dkT, dvT = attend_back(qT, k, kT, v, doT, oT, olo, aux, key_code)
    grad_w_query, grad_w_key, grad_w_value, grad_b_query, grad_b_value = qkv_grad(
        normed, dqT, dkT, dvT
    )
    grad_w_query = halving(grad_w_query, x_first, sizes)
    grad_w_key = halving(grad_w_key, y_first, sizes)
    grad_w_value = halving(grad_w_value, z_first, sizes)
    halves = [
        token_grad(
            h, dqT, dkT, dvT, w_query, w_key, w_value, x, resid_grad, vec(norm1_gain)
        )
        for h in (1, 0)
    ]
    grad_tokens = gather_rows(
        [halves[1 - j // 2][0][j % 2 * local_len : (j % 2 + 1) * local_len] for j in range(seq)]
    )
    grad_gain1 = halves[0][1] + halves[1][1]
    grad_shift1 = halves[0][2] + halves[1][2]

    vectors = [
        grad_gain1,
        grad_shift1,
        grad_b_query,
        grad_b_value,
        grad_b_out,
        grad_gain2,
        grad_shift2,
        grad_b_up,
        grad_b_down,
    ]
    sums = halving(
        jnp.concatenate([g.reshape(rows * seq, -1) for g in vectors], 1), x_first, sizes
    ).reshape(-1)
    parts, start = [], 0
    for g in vectors:
        size = g.size // (rows * seq)
        parts.append(sums[start : start + size])
        start += size
    gain1, shift1, bq, bv, bo, gain2, shift2, bu, bd = parts
    return (
        block_out,
        grad_tokens,
        gain1,
        shift1,
        grad_w_query,
        bq,
        grad_w_key,
        grad_w_value,
        bv,
        grad_w_out,
        bo,
        gain2,
        shift2,
        grad_w_up,
        bu,
        grad_w_down,
        bd,
    )


def solution(mesh):
    tokens = P("rows", "seq", None)
    spread = P(("rows", "seq"))
    spread2 = P(("rows", "seq"), None)
    return jax.shard_map(
        on_device,
        mesh=mesh,
        in_specs=(tokens, P("rows", None), tokens) + (P(),) * 15,
        out_specs=(
            tokens,
            tokens,
            spread,
            spread,
            spread2,
            spread,
            spread2,
            spread2,
            spread,
            spread2,
            spread,
            spread,
            spread,
            spread2,
            spread,
            spread2,
            spread,
        ),
        check_vma=False,
    )
```

time: 1850 us -> 474 us (0.26)
  waiting for transfers between devices: 990 us -> 127 us
  matrix products: 543 us -> 0 us
  Pallas kernels: 0 us -> 198 us
  local copies, waits for them, and re-layouts: 169 us -> 53.3 us
  starting transfers between devices: 0.8 us -> 51.4 us
  other arithmetic: 75.4 us -> 33.2 us
  blocking collectives: 40.7 us -> 0 us
    reduce_scatter x8 -> x0, waiting for transfers between devices: 901 us -> none  [the longest x1 187 us: on_device(): lax.psum_scatter(grad_w_down, ('rows', 'seq'), scatter_dimension=0, tiled...]
    dot_general x74 -> x0, matrix products: 543 us -> none  [the longest x8 107 us: backward_pair(): jnp.einsum('rhqk,rkhe->rqhe', score_low, split_heads(key_pair), preferred...]
    pallas_call x0 -> x10, Pallas kernels: none -> 198 us  [the longest x1 64.6 us: mlp(): pl.pallas_call(mlp_kernel, grid=(hidden // block,), in_specs=[full(), ful...]
    ppermute x0 -> x47, waiting for transfers between devices: none -> 127 us  [swap(): return lax.ppermute(values, axis, [(i, i ^ bit) for i in range(size)])]
    all_gather x2 -> x0, waiting for transfers between devices: 88.4 us -> none  [the longest x1 52.7 us: on_device(): lax.all_gather(key_local, 'seq', axis=1, tiled=True)]
    ppermute x0 -> x47, starting transfers between devices: none -> 51.4 us  [swap(): return lax.ppermute(values, axis, [(i, i ^ bit) for i in range(size)])]
    dynamic_slice x40 -> x5, local copies, waits for them, and re-layouts: 51.2 us -> 4.95 us  [the longest x4 4.93 us: half(): own = lax.dynamic_index_in_dim(kept, which, at, keepdims=False)]
    unnamed x1 -> x0, blocking collectives: 40.7 us -> none
  transfers between devices with their start and end apart: 10 -> 47, of which waited for: 9 -> 20; matrix products, arithmetic and copies ran while one was open for 9% -> 11% of each run, Pallas kernels for 0% -> 12%
where the time goes in v1:
time: 474 us; the launch traced here: 465 us
  Pallas kernels  198 us (42%)
  waiting for transfers between devices  127 us (27%)
  local copies, waits for them, and re-layouts  53.3 us (11%)
  starting transfers between devices  51.4 us (11%)
  other arithmetic  33.2 us (7%)
    ppermute x47, waiting for transfers between devices, swap(): return lax.ppermute(values, axis, [(i, i ^ bit) for i in range(size)])  127 us
    pallas_call x1, Pallas kernels, mlp(): pl.pallas_call(mlp_kernel, grid=(hidden // block,), in_specs=[full(), ful...  64.6 us
    ppermute x47, starting transfers between devices, swap(): return lax.ppermute(values, axis, [(i, i ^ bit) for i in range(size)])  51.4 us
    pallas_call x1, Pallas kernels, attend_back(): pl.pallas_call(attend_back_kernel, grid=(width // 128,), in_specs=[pair,...  47.4 us
    unnamed x106, local copies, waits for them, and re-layouts  25 us
    pallas_call x1, Pallas kernels, attend(): pl.pallas_call(attend_kernel, grid=(width // 128,), in_specs=[pair, pl.Bl...  24.9 us
    pallas_call x2, Pallas kernels, token_grad(): pl.pallas_call(token_grad_kernel, grid=(width // block,), in_specs=[part,...  18.6 us
    convert_element_type x23, other arithmetic, half(): return (own.astype(f32) + other.astype(f32)).astype(values.dtype)  17.7 us
  transfers between devices with their start and end apart: 47, of which 20 were waited for; matrix products, arithmetic and copies ran while one was open for 11% of the time, Pallas kernels for 12%

profile of v1, /device:TPU:0, one launch (start us, length us, event | category | flops | bytes accessed | tf_op | source)
XLA Modules:
  0.0 465.4 jit_solution(3584280883990367595)
XLA Ops:
  0.7 2.7 dynamic-slice_bitcast_fusion.4
  3.8 2.5 collective-permute-start
  6.5 2.1 convert_reduce_fusion
  9.9 1.9 collective-permute-start.4
  18.6 7.9 %shard_map.305 = (bf16[1024,1024]{1,0:T(8,128)(2,1)S(1)}, bf16[1024,1024]{1,0:T(8,128)(2,1)S(1)}, bf16[1024,1024]{1,0:T(8,128)(2,1)S(1)}, bf16[1024,1024]{1,0:T(...) custom-call(bf16[256,1024]{1,0:T(8,128)(2,1)S(1)} %get-tuple-element.155, ...), custom_call_target="tpu_custom_call" | custom-call | flops 3221225472 | bytes 20971520 | tf_op jit(solution)/shard_map/pallas_call | solution.py:83
  26.5 3.7 collective-permute-done.1.refs_1_
  30.2 7.9 %shard_map.306 = (bf16[1024,1024]{1,0:T(8,128)(2,1)S(1)}, bf16[1024,1024]{1,0:T(8,128)(2,1)S(1)}, bf16[1024,1024]{1,0:T(8,128)(2,1)S(1)}, bf16[1024,1024]{1,0:T(...) custom-call(bf16[256,1024]{1,0:T(8,128)(2,1)S(1)} %collective-permut, ...), custom_call_target="tpu_custom_call", output_to_operand_aliasing={{0}: (9, {}), {1}: (10, {}), {2}: (11, {}), {3}: (12, {}), ... | custom-call | flops 3221225472 | bytes 20971520 | tf_op jit(solution)/shard_map/pallas_call | solution.py:83
  44.8 24.9 %shard_map.307 = (bf16[1024,1024]{1,0:T(8,128)(2,1)}, bf16[1024,1024]{1,0:T(8,128)(2,1)}, bf16[1024,1024]{1,0:T(8,128)(2,1)}) custom-call(bf16[1024,1024]{1,0:T(8,128)(2,1)} %copy-done.10, bf16[1024,1024]{1,0:T(8,128)(2,1)} %copy-done.11, bf16[1024,1024]{1,0:T(8,128)(2,1)} %get-tuple-element.82.vT, bf16[64,1024]{1,0:T(8,128)(2,1)} %copy.99.fT, ...), custom_call_target="tpu_custom_call" | custom-call | flops 17179869184 | bytes 12582912 | tf_op jit(solution)/shard_map/pallas_call | solution.py:142
  71.3 4.5 shard_map.308
  77.1 3.5 pad_maximum_fusion.di
  80.6 64.6 %shard_map.309 = (bf16[1024,1024]{1,0:T(8,128)(2,1)}, f32[1024,1024]{1,0:T(8,128)}, bf16[4096,1024]{1,0:T(8,128)(2,1)}, bf16[1024,4096]{1,0:T(8,128)(2,1)}, f32[1,4096]{1,0:T(1,128)}) custom-call(bf16[1024,1024]{1,0:T(8,128)(2,1)} %copy-done.37, bf16[1024,1024]{1,0:T(8,128)(2,1)} %pad_maximum_fusion.di, bf16[1024,4096]{1,0:T(8,128)(2,1)} %wu.1, ...), custom_call_target="tpu_custom_call" | custom-call | flops 51539607552 | bytes 52428800 | tf_op jit(solution)/shard_map/pallas_call | solution.py:271
  145.2 11.3 %shard_map.310 = (bf16[1024,1024]{1,0:T(8,128)(2,1)S(1)}, f32[1024,1024]{1,0:T(8,128)}, bf16[1024,1024]{1,0:T(8,128)(2,1)S(1)}, f32[1,1024]{1,0:T(1,128)S(1)}, f...) custom-call(f32[1024,1024]{1,0:T(8,128)} %get-tuple-element.90.dn, f32[1024,1024]{1,0:T(8,128)} %copy-done.33, ...), custom_call_target="tpu_custom_call" | custom-call | flops 4294967296 | bytes 25165824 | tf_op jit(solution)/shard_map/pallas_call | solution.py:327
  159.1 47.4 %shard_map.311 = (bf16[1024,1024]{1,0:T(8,128)(2,1)}, bf16[1024,1024]{1,0:T(8,128)(2,1)}, bf16[1024,1024]{1,0:T(8,128)(2,1)}) custom-call(bf16[1024,1024]{1,0:T(8,128)(2,1)} %copy-done.10, bf16[1024,1024]{1,0:T(8,128)(2,1)} %copy-done.11, bf16[1024,1024]{1,0:T(8,128)(2,1)} %copy-done.12, bf16[1024,1024]{1,0:T(8,128)(2,1)} %copy-done.13, ...), custom_call_target="tpu_custom_call" | custom-call | flops 42949672960 | bytes 23068672 | tf_op jit(solution)/shard_map/pallas_call | solution.py:189
  208.2 1.6 copy-done.5
  209.8 1.6 copy-done.7
  211.4 9.3 %shard_map.313 = (bf16[512,1024]{1,0:T(8,128)(2,1)S(1)}, f32[1,1024]{1,0:T(1,128)S(1)}, f32[1,1024]{1,0:T(1,128)S(1)}) custom-call(bf16[1024,1024]{1,0:T(8,128)(2,1)S(1)} %copy-done.4, bf16[1024,1024]{1,0:T(8,128)(2,1)S(1)} %copy-done.5, bf16[1024,1024]{1,0:T(8,128)(2,1)S(1)} %copy-done.7, bf16[1024,1024]{1,0:T(8,128)(2,1)S(1)} %copy-done, ...), custom_call_target="tpu_custom_call" | custom-call | flops 3221225472 | bytes 14680064 | tf_op jit(solution)/shard_map/pallas_call | solution.py:407
  220.7 9.3 %shard_map.312 = (bf16[512,1024]{1,0:T(8,128)(2,1)S(1)}, f32[1,1024]{1,0:T(1,128)S(1)}, f32[1,1024]{1,0:T(1,128)S(1)}) custom-call(bf16[1024,1024]{1,0:T(8,128)(2,1)S(1)} %copy-done.4, bf16[1024,1024]{1,0:T(8,128)(2,1)S(1)} %copy-done.5, bf16[1024,1024]{1,0:T(8,128)(2,1)S(1)} %copy-done.7, bf16[1024,1024]{1,0:T(8,128)(2,1)S(1)} %copy-done, ...), custom_call_target="tpu_custom_call" | custom-call | flops 3221225472 | bytes 14680064 | tf_op jit(solution)/shard_map/pallas_call | solution.py:407
  230.0 2.6 copy_bitcast_fusion
  232.9 4.8 %copy_bitcast_fusion.1 = bf16[2,2,2,2,32,4096]{5,4,3,2,0,1:T(8,128)(2,1)} fusion(bf16[2,2,2,2,2,32,4096]{6,5,4,3,2,1,0:T(8,128)(2,1)} %bitcast.414, s32[]{:T(128)S(6)} %select_n.420), kind=kLoop, calls=%fused_computation.9 | loop fusion | bytes 8388612 | tf_op jit(solution)/shard_map/jit(dynamic_index_in_dim)/squeeze | solution.py:438
  238.0 10.6 %shard_map.314 = (bf16[1024,1024]{1,0:T(8,128)(2,1)S(1)}, bf16[1024,1024]{1,0:T(8,128)(2,1)S(1)}, bf16[1024,1024]{1,0:T(8,128)(2,1)S(1)}, f32[1,1024]{1,0:T(1,128)S(1)}, f32[1,1024]{1,0:T(1,128)S(1)}) custom-call(bf16[1024,1024]{1,0:T(8,128)(2,1)S(1)} %copy-done.9, bf16[1024,1024]{1,0:T(8,128)(2,1)S(1)} %copy-done.4, bf16[1024,1024]{1,0:T(8,128)(2,1)S(1)} %copy-done.6, ...), custom_call_target="tpu_custom_call" | custom-call | flops 6442450944 | bytes 14680064 | tf_op jit(solution)/shard_map/pallas_call | solution.py:364
  256.4 2.0 collective-permute-start.10
  259.5 2.8 constant_dynamic-slice_fusion.1
  273.2 1.7 collective-permute-done.14
  274.9 1.6 collective-permute-start.15
  278.6 2.6 collective-permute-start.16
  285.4 11.9 %collective-permute-done.11 = bf16[256,1024]{1,0:T(8,128)(2,1)S(1)} collective-permute-done((bf16[256,1024]{1,0:T(8,128)(2,1)S(1)}, bf16[256,1024]{1,0:T(8,128)(2,1)S(1)}, u32[]{:S(2)}, u32[]{:S(2)}) %collective-permute-start.11) | collective-permute-done | bytes 524320 | tf_op jit(solution)/shard_map/ppermute | solution.py:420
  299.2 4.0 fusion.3
  303.4 4.5 fusion.1
  310.4 1.6 collective-permute-start.38
  311.9 1.6 fusion.15
  313.6 1.7 fusion.11
  315.3 6.9 %collective-permute-done.7 = bf16[256,1024]{1,0:T(8,128)(2,1)S(1)} collective-permute-done((bf16[256,1024]{1,0:T(8,128)(2,1)S(1)}, bf16[256,1024]{1,0:T(8,128)(2,1)S(1)}, u32[]{:S(2)}, u32[]{:S(2)}) %collective-permute-start.7) | collective-permute-done | bytes 524320 | tf_op jit(solution)/shard_map/ppermute | solution.py:420
  325.8 1.6 fusion.13
  327.4 9.6 %collective-permute-done.23 = bf16[2,2,2,32,1024]{4,3,0,2,1:T(8,128)(2,1)S(1)} collective-permute-done((bf16[2,2,2,32,1024]{4,3,0,2,1:T(8,128)(2,1)S(1)}, bf16[2,2,2,32,1024]{4,3,0,2,1:T(8,128)(2,1)S(1)}, u32[]{:S(2)}, u32[]{:S(2)}) %collective-permute-start.23) | collective-permute-done | bytes 524320 | tf_op jit(solution)/shard_map/ppermute | solution.py:420
  337.1 1.6 collective-permute-start.28
  338.6 9.6 %collective-permute-done.33 = bf16[2,2,2,32,1024]{4,3,0,2,1:T(8,128)(2,1)S(1)} collective-permute-done((bf16[2,2,2,32,1024]{4,3,0,2,1:T(8,128)(2,1)S(1)}, bf16[2,2,2,32,1024]{4,3,0,2,1:T(8,128)(2,1)S(1)}, u32[]{:S(2)}, u32[]{:S(2)}) %collective-permute-start.33) | collective-permute-done | bytes 524320 | tf_op jit(solution)/shard_map/ppermute | solution.py:420
  350.3 6.3 %collective-permute-done.8 = bf16[256,1024]{1,0:T(8,128)(2,1)S(1)} collective-permute-done((bf16[256,1024]{1,0:T(8,128)(2,1)S(1)}, bf16[256,1024]{1,0:T(8,128)(2,1)S(1)}, u32[]{:S(2)}, u32[]{:S(2)}) %collective-permute-start.8) | collective-permute-done | bytes 524320 | tf_op jit(solution)/shard_map/ppermute | solution.py:420
  358.2 10.8 %collective-permute-done.28 = bf16[2,2,2,32,1024]{4,3,2,1,0:T(8,128)(2,1)S(1)} collective-permute-done((bf16[2,2,2,32,1024]{4,3,2,1,0:T(8,128)(2,1)S(1)}, bf16[2,2,2,32,1024]{4,3,2,1,0:T(8,128)(2,1)S(1)}, u32[]{:S(2)}, u32[]{:S(2)}) %collective-permute-start.28) | collective-permute-done | bytes 524320 | tf_op jit(solution)/shard_map/ppermute | solution.py:420
  369.1 2.4 collective-permute-start.29
  375.2 1.7 collective-permute-start.35
  379.6 3.4 collective-permute-done.29
  384.1 3.6 collective-permute-start.25
  388.1 2.9 collective-permute-start.36
  391.0 18.4 %collective-permute-done.25 = bf16[2,32,1024]{2,1,0:T(8,128)(2,1)S(1)} collective-permute-done((bf16[2,32,1024]{2,1,0:T(8,128)(2,1)S(1)}, bf16[2,32,1024]{2,1,0:T(8,128)(2,1)S(1)}, u32[]{:S(2)}, u32[]{:S(2)}) %collective-permute-start.25) | collective-permute-done | bytes 131104 | tf_op jit(solution)/shard_map/ppermute | solution.py:420
  411.1 5.5 %collective-permute-start.26 = (bf16[32,1024]{1,0:T(8,128)(2,1)S(1)}, bf16[32,1024]{1,0:T(8,128)(2,1)S(1)}, u32[]{:S(2)}, u32[]{:S(2)}) collective-permute-start(bf16[32,1024]{1,0:T(8,128)(2,1)S(1)} %fusion.57), channel_id=1, source_target_pairs={{0,16},{4,20},{8,24},{12,28},{16,0},{20,4},{24,8},{28,12},{1,17},{... | collective-permute-start | bytes 196616 | tf_op jit(solution)/shard_map/ppermute | solution.py:420
  416.5 18.6 %collective-permute-done.36 = bf16[32,1024]{1,0:T(8,128)(2,1)S(1)} collective-permute-done((bf16[32,1024]{1,0:T(8,128)(2,1)S(1)}, bf16[32,1024]{1,0:T(8,128)(2,1)S(1)}, u32[]{:S(2)}, u32[]{:S(2)}) %collective-permute-start.36) | collective-permute-done | bytes 65568 | tf_op jit(solution)/shard_map/ppermute | solution.py:420
  439.7 10.4 %collective-permute-done.45 = bf16[2,128,1024]{2,1,0:T(8,128)(2,1)S(1)} collective-permute-done((bf16[2,128,1024]{2,1,0:T(8,128)(2,1)S(1)}, bf16[2,128,1024]{2,1,0:T(8,128)(2,1)S(1)}, u32[]{:S(2)}, u32[]{:S(2)}) %collective-permute-start.45) | collective-permute-done | bytes 524320 | tf_op jit(solution)/shard_map/ppermute | solution.py:420
  453.0 10.4 %collective-permute-done.46 = bf16[128,1024]{1,0:T(8,128)(2,1)S(1)} collective-permute-done((bf16[128,1024]{1,0:T(8,128)(2,1)S(1)}, bf16[128,1024]{1,0:T(8,128)(2,1)S(1)}, u32[]{:S(2)}, u32[]{:S(2)}) %collective-permute-start.46) | collective-permute-done | bytes 262176 | tf_op jit(solution)/shard_map/ppermute | solution.py:420
  (269 shorter events, 78.0 us)
Async XLA Ops:
  3.4 13.3 %collective-permute-start.2 = (bf16[256,1024]{1,0:T(8,128)(2,1)}, bf16[256,1024]{1,0:T(8,128)(2,1)S(1)}, u32[]{:S(2)}, u32[]{:S(2)}) collective-permute-start(bf16[256,1024]{1,0:T(8,128)(2,1)} %get-tuple-element.152), channel_id=1, source_target_pairs={{0,1},{1,0},{2,3},{3,2},{4,5},{5,4},{6,7},{7,6},{8,9},{9,8},{10,11... | collective-permute-start | bytes 1572872 | tf_op jit(solution)/shard_map/ppermute | solution.py:420
  3.8 22.7 %collective-permute-start = (bf16[256,1024]{1,0:T(8,128)(2,1)}, bf16[256,1024]{1,0:T(8,128)(2,1)S(1)}, u32[]{:S(2)}, u32[]{:S(2)}) collective-permute-start(bf16[256,1024]{1,0:T(8,128)(2,1)} %get-tuple-element.154), channel_id=1, source_target_pairs={{0,2},{1,3},{2,0},{3,1},{4,6},{5,7},{6,4},{7,5},{8,10},{9,11},{10,... | collective-permute-start | bytes 1572872 | tf_op jit(solution)/shard_map/ppermute | solution.py:420
  6.4 23.9 %collective-permute-start.1 = (bf16[256,1024]{1,0:T(8,128)(2,1)}, bf16[256,1024]{1,0:T(8,128)(2,1)S(1)}, u32[]{:S(2)}, u32[]{:S(2)}) collective-permute-start(bf16[256,1024]{1,0:T(8,128)(2,1)} %get-tuple-element.153), channel_id=1, source_target_pairs={{0,3},{1,2},{2,1},{3,0},{4,7},{5,6},{6,5},{7,4},{8,11},{9,10},{10,... | collective-permute-start | bytes 1572872 | tf_op jit(solution)/shard_map/ppermute | solution.py:420
  9.8 67.3 %collective-permute-start.3 = (bf16[256,1024]{1,0:T(8,128)(2,1)}, bf16[256,1024]{1,0:T(8,128)(2,1)}, u32[]{:S(2)}, u32[]{:S(2)}) collective-permute-start(bf16[256,1024]{1,0:T(8,128)(2,1)} %get-tuple-element.151), channel_id=1, source_target_pairs={{0,1},{1,0},{2,3},{3,2},{4,5},{5,4},{6,7},{7,6},{8,9},{9,8},{10,11... | collective-permute-start | bytes 1572872 | tf_op jit(solution)/shard_map/ppermute | solution.py:420
  9.9 67.2 %collective-permute-start.4 = (bf16[256,1024]{1,0:T(8,128)(2,1)}, bf16[256,1024]{1,0:T(8,128)(2,1)}, u32[]{:S(2)}, u32[]{:S(2)}) collective-permute-start(bf16[256,1024]{1,0:T(8,128)(2,1)} %get-tuple-element.150), channel_id=1, source_target_pairs={{0,2},{1,3},{2,0},{3,1},{4,6},{5,7},{6,4},{7,5},{8,10},{9,11},{10,... | collective-permute-start | bytes 1572872 | tf_op jit(solution)/shard_map/ppermute | solution.py:420
  17.5 59.6 %collective-permute-start.5 = (bf16[256,1024]{1,0:T(8,128)(2,1)}, bf16[256,1024]{1,0:T(8,128)(2,1)S(1)}, u32[]{:S(2)}, u32[]{:S(2)}) collective-permute-start(bf16[256,1024]{1,0:T(8,128)(2,1)} %get-tuple-element.149), channel_id=1, source_target_pairs={{0,3},{1,2},{2,1},{3,0},{4,7},{5,6},{6,5},{7,4},{8,11},{9,10},{10,... | collective-permute-start | bytes 1572872 | tf_op jit(solution)/shard_map/ppermute | solution.py:420
  80.6 64.6 %copy-start.35 = (bf16[1024,1024]{1,0:T(8,128)(2,1)S(1)}, bf16[1024,1024]{1,0:T(8,128)(2,1)}, u32[]{:S(2)}) copy-start(bf16[1024,1024]{1,0:T(8,128)(2,1)} %get-tuple-element.83.oT) | copy-start | bytes 6291460
  232.7 70.5 %collective-permute-start.42 = (bf16[2,2,2,2,128,1024]{5,4,0,3,1,2:T(8,128)(2,1)}, bf16[2,2,2,2,128,1024]{5,4,0,3,1,2:T(8,128)(2,1)}, u32[]{:S(2)}, u32[]{:S(2)}) collective-permute-start(bf16[2,2,2,2,128,1024]{5,4,0,3,1,2:T(8,128)(2,1)} %copy_bitcast_fusion), channel_id=1, source_target_pairs={{0,1},{1,0},{2,3},{3,2},{4,5},{5,4},{6,7},{7,6},{8,9},{9,8},{10,11... | collective-permute-start | bytes 12582920 | tf_op jit(solution)/shard_map/ppermute | solution.py:420
  237.7 59.8 %collective-permute-start.37 = (bf16[2,2,2,2,32,4096]{5,4,3,2,0,1:T(8,128)(2,1)}, bf16[2,2,2,2,32,4096]{5,4,3,2,0,1:T(8,128)(2,1)}, u32[]{:S(2)}, u32[]{:S(2)}) collective-permute-start(bf16[2,2,2,2,32,4096]{5,4,3,2,0,1:T(8,128)(2,1)} %copy_bitcast_fusion.1), channel_id=1, source_target_pairs={{0,1},{1,0},{2,3},{3,2},{4,5},{5,4},{6,7},{7,6},{8,9},{9,8},{10,11... | collective-permute-start | bytes 12582920 | tf_op jit(solution)/shard_map/ppermute | solution.py:420
  256.1 11.3 %collective-permute-start.12 = (f32[2,2,2,2,1,384]{5,4,3,2,1,0:T(1,128)S(1)}, f32[2,2,2,2,1,384]{5,4,3,2,1,0:T(1,128)S(1)}, u32[]{:S(2)}, u32[]{:S(2)}) collective-permute-start(f32[2,2,2,2,1,384]{5,4,3,2,1,0:T(1,128)S(1)} %fusion.62), channel_id=1, source_target_pairs={{0,1},{1,0},{2,3},{3,2},{4,5},{5,4},{6,7},{7,6},{8,9},{9,8},{10,11... | collective-permute-start | bytes 73736 | tf_op jit(solution)/shard_map/ppermute | solution.py:420
  256.4 28.8 %collective-permute-start.10 = (bf16[256,1024]{1,0:T(8,128)(2,1)S(1)}, bf16[256,1024]{1,0:T(8,128)(2,1)S(1)}, u32[]{:S(2)}, u32[]{:S(2)}) collective-permute-start(bf16[256,1024]{1,0:T(8,128)(2,1)S(1)} %get-tuple-element.171), channel_id=1, source_target_pairs={{0,2},{1,3},{2,0},{3,1},{4,6},{5,7},{6,4},{7,5},{8,10},{9,11},{10,... | collective-permute-start | bytes 1572872 | tf_op jit(solution)/shard_map/ppermute | solution.py:420
  267.4 3.8 collective-permute-start.13
  271.2 3.7 collective-permute-start.14
  274.9 3.7 collective-permute-start.15
  278.6 4.5 collective-permute-start.16
  282.3 2.2 collective-permute-start.9
  283.1 14.2 %collective-permute-start.11 = (bf16[256,1024]{1,0:T(8,128)(2,1)S(1)}, bf16[256,1024]{1,0:T(8,128)(2,1)S(1)}, u32[]{:S(2)}, u32[]{:S(2)}) collective-permute-start(bf16[256,1024]{1,0:T(8,128)(2,1)S(1)} %get-tuple-element.170), channel_id=1, source_target_pairs={{0,3},{1,2},{2,1},{3,0},{4,7},{5,6},{6,5},{7,4},{8,11},{9,10},{10,... | collective-permute-start | bytes 1572872 | tf_op jit(solution)/shard_map/ppermute | solution.py:420
  284.5 24.3 %collective-permute-start.22 = (bf16[2,2,2,2,32,1024]{5,4,0,2,1,3:T(8,128)(2,1)}, bf16[2,2,2,2,32,1024]{5,4,0,2,1,3:T(8,128)(2,1)}, u32[]{:S(2)}, u32[]{:S(2)}) collective-permute-start(bf16[2,2,2,2,32,1024]{5,4,0,2,1,3:T(8,128)(2,1)} %copy_bitcast_fusion.6), channel_id=1, source_target_pairs={{0,1},{1,0},{2,3},{3,2},{4,5},{5,4},{6,7},{7,6},{8,9},{9,8},{10,11... | collective-permute-start | bytes 3145736 | tf_op jit(solution)/shard_map/ppermute | solution.py:420
  285.3 25.1 %collective-permute-start.32 = (bf16[2,2,2,2,32,1024]{5,4,0,2,1,3:T(8,128)(2,1)}, bf16[2,2,2,2,32,1024]{5,4,0,2,1,3:T(8,128)(2,1)}, u32[]{:S(2)}, u32[]{:S(2)}) collective-permute-start(bf16[2,2,2,2,32,1024]{5,4,0,2,1,3:T(8,128)(2,1)} %copy_bitcast_fusion.4), channel_id=1, source_target_pairs={{0,1},{1,0},{2,3},{3,2},{4,5},{5,4},{6,7},{7,6},{8,9},{9,8},{10,11... | collective-permute-start | bytes 3145736 | tf_op jit(solution)/shard_map/ppermute | solution.py:420
  297.3 25.8 %collective-permute-start.27 = (bf16[2,2,2,2,32,1024]{5,4,3,2,0,1:T(8,128)(2,1)}, bf16[2,2,2,2,32,1024]{5,4,3,2,0,1:T(8,128)(2,1)}, u32[]{:S(2)}, u32[]{:S(2)}) collective-permute-start(bf16[2,2,2,2,32,1024]{5,4,3,2,0,1:T(8,128)(2,1)} %copy_bitcast_fusion.5), channel_id=1, source_target_pairs={{0,1},{1,0},{2,3},{3,2},{4,5},{5,4},{6,7},{7,6},{8,9},{9,8},{10,11... | collective-permute-start | bytes 3145736 | tf_op jit(solution)/shard_map/ppermute | solution.py:420
  298.7 9.1 %collective-permute-start.6 = (bf16[256,1024]{1,0:T(8,128)(2,1)}, bf16[256,1024]{1,0:T(8,128)(2,1)}, u32[]{:S(2)}, u32[]{:S(2)}) collective-permute-start(bf16[256,1024]{1,0:T(8,128)(2,1)} %get-tuple-element.147), channel_id=1, source_target_pairs={{0,1},{1,0},{2,3},{3,2},{4,5},{5,4},{6,7},{7,6},{8,9},{9,8},{10,11... | collective-permute-start | bytes 1572872 | tf_op jit(solution)/shard_map/ppermute | solution.py:420
  303.2 22.1 %collective-permute-start.17 = (bf16[2,2,2,2,32,1024]{5,4,0,3,1,2:T(8,128)(2,1)}, bf16[2,2,2,2,32,1024]{5,4,0,3,1,2:T(8,128)(2,1)S(1)}, u32[]{:S(2)}, u32[]{:S(2)}) collective-permute-start(bf16[2,2,2,2,32,1024]{5,4,0,3,1,2:T(8,128)(2,1)} %copy_bitcast_fusion.7), channel_id=1, source_target_pairs={{0,1},{1,0},{2,3},{3,2},{4,5},{5,4},{6,7},{7,6},{8,9},{9,8},{10,11... | collective-permute-start | bytes 3145736 | tf_op jit(solution)/shard_map/ppermute | solution.py:420
  307.9 14.3 %collective-permute-start.7 = (bf16[256,1024]{1,0:T(8,128)(2,1)S(1)}, bf16[256,1024]{1,0:T(8,128)(2,1)S(1)}, u32[]{:S(2)}, u32[]{:S(2)}) collective-permute-start(bf16[256,1024]{1,0:T(8,128)(2,1)S(1)} %copy-done.45), channel_id=1, source_target_pairs={{0,2},{1,3},{2,0},{3,1},{4,6},{5,7},{6,4},{7,5},{8,10},{9,11},{10,... | collective-permute-start | bytes 1572872 | tf_op jit(solution)/shard_map/ppermute | solution.py:420
  308.9 66.3 %collective-permute-start.43 = (bf16[2,2,2,128,1024]{4,3,0,2,1:T(8,128)(2,1)S(1)}, bf16[2,2,2,128,1024]{4,3,0,2,1:T(8,128)(2,1)S(1)}, u32[]{:S(2)}, u32[]{:S(2)}) collective-permute-start(bf16[2,2,2,128,1024]{4,3,0,2,1:T(8,128)(2,1)S(1)} %get-tuple-element.130), channel_id=1, source_target_pairs={{0,4},{4,0},{8,12},{12,8},{16,20},{20,16},{24,28},{28,24},{1,5},{5... | collective-permute-start | bytes 6291464 | tf_op jit(solution)/shard_map/ppermute | solution.py:420
  310.4 67.8 %collective-permute-start.38 = (bf16[2,2,2,32,4096]{4,3,2,1,0:T(8,128)(2,1)S(1)}, bf16[2,2,2,32,4096]{4,3,2,1,0:T(8,128)(2,1)S(1)}, u32[]{:S(2)}, u32[]{:S(2)}) collective-permute-start(bf16[2,2,2,32,4096]{4,3,2,1,0:T(8,128)(2,1)S(1)} %get-tuple-element.124), channel_id=1, source_target_pairs={{0,8},{4,12},{8,0},{12,4},{16,24},{20,28},{24,16},{28,20},{1,9},{5... | collective-permute-start | bytes 6291464 | tf_op jit(solution)/shard_map/ppermute | solution.py:420
  322.2 14.8 %collective-permute-start.23 = (bf16[2,2,2,32,1024]{4,3,0,2,1:T(8,128)(2,1)S(1)}, bf16[2,2,2,32,1024]{4,3,0,2,1:T(8,128)(2,1)S(1)}, u32[]{:S(2)}, u32[]{:S(2)}) collective-permute-start(bf16[2,2,2,32,1024]{4,3,0,2,1:T(8,128)(2,1)S(1)} %get-tuple-element.165), channel_id=1, source_target_pairs={{0,2},{1,3},{2,0},{3,1},{4,6},{5,7},{6,4},{7,5},{8,10},{9,11},{10,... | collective-permute-start | bytes 1572872 | tf_op jit(solution)/shard_map/ppermute | solution.py:420
  323.1 25.2 %collective-permute-start.33 = (bf16[2,2,2,32,1024]{4,3,0,2,1:T(8,128)(2,1)S(1)}, bf16[2,2,2,32,1024]{4,3,0,2,1:T(8,128)(2,1)S(1)}, u32[]{:S(2)}, u32[]{:S(2)}) collective-permute-start(bf16[2,2,2,32,1024]{4,3,0,2,1:T(8,128)(2,1)S(1)} %get-tuple-element.159), channel_id=1, source_target_pairs={{0,2},{1,3},{2,0},{3,1},{4,6},{5,7},{6,4},{7,5},{8,10},{9,11},{10,... | collective-permute-start | bytes 1572872 | tf_op jit(solution)/shard_map/ppermute | solution.py:420
  325.3 31.3 %collective-permute-start.8 = (bf16[256,1024]{1,0:T(8,128)(2,1)S(1)}, bf16[256,1024]{1,0:T(8,128)(2,1)S(1)}, u32[]{:S(2)}, u32[]{:S(2)}) collective-permute-start(bf16[256,1024]{1,0:T(8,128)(2,1)S(1)} %copy-done.44), channel_id=1, source_target_pairs={{0,3},{1,2},{2,1},{3,0},{4,7},{5,6},{6,5},{7,4},{8,11},{9,10},{10,... | collective-permute-start | bytes 1572872 | tf_op jit(solution)/shard_map/ppermute | solution.py:420
  337.1 31.9 %collective-permute-start.28 = (bf16[2,2,2,32,1024]{4,3,2,1,0:T(8,128)(2,1)S(1)}, bf16[2,2,2,32,1024]{4,3,2,1,0:T(8,128)(2,1)S(1)}, u32[]{:S(2)}, u32[]{:S(2)}) collective-permute-start(bf16[2,2,2,32,1024]{4,3,2,1,0:T(8,128)(2,1)S(1)} %get-tuple-element.134), channel_id=1, source_target_pairs={{0,8},{4,12},{8,0},{12,4},{16,24},{20,28},{24,16},{28,20},{1,9},{5... | collective-permute-start | bytes 1572872 | tf_op jit(solution)/shard_map/ppermute | solution.py:420
  348.3 23.3 %collective-permute-start.18 = (bf16[2,2,2,32,1024]{4,3,0,2,1:T(8,128)(2,1)S(1)}, bf16[2,2,2,32,1024]{4,3,0,2,1:T(8,128)(2,1)S(1)}, u32[]{:S(2)}, u32[]{:S(2)}) collective-permute-start(bf16[2,2,2,32,1024]{4,3,0,2,1:T(8,128)(2,1)S(1)} %get-tuple-element.169), channel_id=1, source_target_pairs={{0,4},{4,0},{8,12},{12,8},{16,20},{20,16},{24,28},{28,24},{1,5},{5... | collective-permute-start | bytes 1572872 | tf_op jit(solution)/shard_map/ppermute | solution.py:420
  356.6 17.0 %collective-permute-start.34 = (bf16[2,2,32,1024]{3,2,1,0:T(8,128)(2,1)S(1)}, bf16[2,2,32,1024]{3,2,1,0:T(8,128)(2,1)S(1)}, u32[]{:S(2)}, u32[]{:S(2)}) collective-permute-start(bf16[2,2,32,1024]{3,2,1,0:T(8,128)(2,1)S(1)} %copy.116), channel_id=1, source_target_pairs={{0,4},{4,0},{8,12},{12,8},{16,20},{20,16},{24,28},{28,24},{1,5},{5... | collective-permute-start | bytes 786440 | tf_op jit(solution)/shard_map/ppermute | solution.py:420
  369.1 13.8 %collective-permute-start.29 = (bf16[2,2,32,1024]{3,2,1,0:T(8,128)(2,1)S(1)}, bf16[2,2,32,1024]{3,2,1,0:T(8,128)(2,1)S(1)}, u32[]{:S(2)}, u32[]{:S(2)}) collective-permute-start(bf16[2,2,32,1024]{3,2,1,0:T(8,128)(2,1)S(1)} %get-tuple-element.161), channel_id=1, source_target_pairs={{0,16},{4,20},{8,24},{12,28},{16,0},{20,4},{24,8},{28,12},{1,17},{... | collective-permute-start | bytes 786440 | tf_op jit(solution)/shard_map/ppermute | solution.py:420
  371.6 11.5 %collective-permute-start.24 = (bf16[2,2,32,1024]{3,2,1,0:T(8,128)(2,1)S(1)}, bf16[2,2,32,1024]{3,2,1,0:T(8,128)(2,1)S(1)}, u32[]{:S(2)}, u32[]{:S(2)}) collective-permute-start(bf16[2,2,32,1024]{3,2,1,0:T(8,128)(2,1)S(1)} %copy.108), channel_id=1, source_target_pairs={{0,4},{4,0},{8,12},{12,8},{16,20},{20,16},{24,28},{28,24},{1,5},{5... | collective-permute-start | bytes 786440 | tf_op jit(solution)/shard_map/ppermute | solution.py:420
  373.6 10.5 %collective-permute-start.19 = (bf16[2,2,32,1024]{3,2,1,0:T(8,128)(2,1)S(1)}, bf16[2,2,32,1024]{3,2,1,0:T(8,128)(2,1)S(1)}, u32[]{:S(2)}, u32[]{:S(2)}) collective-permute-start(bf16[2,2,32,1024]{3,2,1,0:T(8,128)(2,1)S(1)} %copy.103), channel_id=1, source_target_pairs={{0,2},{1,3},{2,0},{3,1},{4,6},{5,7},{6,4},{7,5},{8,10},{9,11},{10,... | collective-permute-start | bytes 786440 | tf_op jit(solution)/shard_map/ppermute | solution.py:420
  375.2 12.6 %collective-permute-start.35 = (bf16[2,32,1024]{2,1,0:T(8,128)(2,1)S(1)}, bf16[2,32,1024]{2,1,0:T(8,128)(2,1)S(1)}, u32[]{:S(2)}, u32[]{:S(2)}) collective-permute-start(bf16[2,32,1024]{2,1,0:T(8,128)(2,1)S(1)} %get-tuple-element.173), channel_id=1, source_target_pairs={{0,8},{4,12},{8,0},{12,4},{16,24},{20,28},{24,16},{28,20},{1,9},{5... | collective-permute-start | bytes 393224 | tf_op jit(solution)/shard_map/ppermute | solution.py:420
  378.2 57.7 %collective-permute-start.44 = (bf16[2,2,128,1024]{3,2,1,0:T(8,128)(2,1)S(1)}, bf16[2,2,128,1024]{3,2,1,0:T(8,128)(2,1)S(1)}, u32[]{:S(2)}, u32[]{:S(2)}) collective-permute-start(bf16[2,2,128,1024]{3,2,1,0:T(8,128)(2,1)S(1)} %copy.124), channel_id=1, source_target_pairs={{0,2},{1,3},{2,0},{3,1},{4,6},{5,7},{6,4},{7,5},{8,10},{9,11},{10,... | collective-permute-start | bytes 3145736 | tf_op jit(solution)/shard_map/ppermute | solution.py:420
  383.0 54.5 %collective-permute-start.39 = (bf16[2,2,32,4096]{3,2,1,0:T(8,128)(2,1)S(1)}, bf16[2,2,32,4096]{3,2,1,0:T(8,128)(2,1)S(1)}, u32[]{:S(2)}, u32[]{:S(2)}) collective-permute-start(bf16[2,2,32,4096]{3,2,1,0:T(8,128)(2,1)S(1)} %get-tuple-element.132), channel_id=1, source_target_pairs={{0,16},{4,20},{8,24},{12,28},{16,0},{20,4},{24,8},{28,12},{1,17},{... | collective-permute-start | bytes 3145736 | tf_op jit(solution)/shard_map/ppermute | solution.py:420
  383.0 5.0 %collective-permute-start.30 = (bf16[2,32,1024]{2,1,0:T(8,128)(2,1)S(1)}, bf16[2,32,1024]{2,1,0:T(8,128)(2,1)S(1)}, u32[]{:S(2)}, u32[]{:S(2)}) collective-permute-start(bf16[2,32,1024]{2,1,0:T(8,128)(2,1)S(1)} %get-tuple-element.175), channel_id=1, source_target_pairs={{0,4},{4,0},{8,12},{12,8},{16,20},{20,16},{24,28},{28,24},{1,5},{5... | collective-permute-start | bytes 393224 | tf_op jit(solution)/shard_map/ppermute | solution.py:420
  384.1 25.3 %collective-permute-start.25 = (bf16[2,32,1024]{2,1,0:T(8,128)(2,1)S(1)}, bf16[2,32,1024]{2,1,0:T(8,128)(2,1)S(1)}, u32[]{:S(2)}, u32[]{:S(2)}) collective-permute-start(bf16[2,32,1024]{2,1,0:T(8,128)(2,1)S(1)} %get-tuple-element.177), channel_id=1, source_target_pairs={{0,8},{4,12},{8,0},{12,4},{16,24},{20,28},{24,16},{28,20},{1,9},{5... | collective-permute-start | bytes 393224 | tf_op jit(solution)/shard_map/ppermute | solution.py:420
  387.8 23.2 %collective-permute-start.20 = (bf16[2,32,1024]{2,1,0:T(8,128)(2,1)S(1)}, bf16[2,32,1024]{2,1,0:T(8,128)(2,1)S(1)}, u32[]{:S(2)}, u32[]{:S(2)}) collective-permute-start(bf16[2,32,1024]{2,1,0:T(8,128)(2,1)S(1)} %get-tuple-element.179), channel_id=1, source_target_pairs={{0,8},{4,12},{8,0},{12,4},{16,24},{20,28},{24,16},{28,20},{1,9},{5... | collective-permute-start | bytes 393224 | tf_op jit(solution)/shard_map/ppermute | solution.py:420
  388.1 47.1 %collective-permute-start.36 = (bf16[32,1024]{1,0:T(8,128)(2,1)S(1)}, bf16[32,1024]{1,0:T(8,128)(2,1)S(1)}, u32[]{:S(2)}, u32[]{:S(2)}) collective-permute-start(bf16[32,1024]{1,0:T(8,128)(2,1)S(1)} %fusion.61), channel_id=1, source_target_pairs={{0,16},{4,20},{8,24},{12,28},{16,0},{20,4},{24,8},{28,12},{1,17},{... | collective-permute-start | bytes 196616 | tf_op jit(solution)/shard_map/ppermute | solution.py:420
  409.4 28.9 %collective-permute-start.31 = (bf16[32,1024]{1,0:T(8,128)(2,1)S(1)}, bf16[32,1024]{1,0:T(8,128)(2,1)S(1)}, u32[]{:S(2)}, u32[]{:S(2)}) collective-permute-start(bf16[32,1024]{1,0:T(8,128)(2,1)S(1)} %fusion.59), channel_id=1, source_target_pairs={{0,2},{1,3},{2,0},{3,1},{4,6},{5,7},{6,4},{7,5},{8,10},{9,11},{10,... | collective-permute-start | bytes 196616 | tf_op jit(solution)/shard_map/ppermute | solution.py:420
  411.1 27.9 %collective-permute-start.26 = (bf16[32,1024]{1,0:T(8,128)(2,1)S(1)}, bf16[32,1024]{1,0:T(8,128)(2,1)S(1)}, u32[]{:S(2)}, u32[]{:S(2)}) collective-permute-start(bf16[32,1024]{1,0:T(8,128)(2,1)S(1)} %fusion.57), channel_id=1, source_target_pairs={{0,16},{4,20},{8,24},{12,28},{16,0},{20,4},{24,8},{28,12},{1,17},{... | collective-permute-start | bytes 196616 | tf_op jit(solution)/shard_map/ppermute | solution.py:420
  435.2 17.1 %collective-permute-start.21 = (bf16[32,1024]{1,0:T(8,128)(2,1)S(1)}, bf16[32,1024]{1,0:T(8,128)(2,1)S(1)}, u32[]{:S(2)}, u32[]{:S(2)}) collective-permute-start(bf16[32,1024]{1,0:T(8,128)(2,1)S(1)} %fusion.55), channel_id=1, source_target_pairs={{0,16},{4,20},{8,24},{12,28},{16,0},{20,4},{24,8},{28,12},{1,17},{... | collective-permute-start | bytes 196616 | tf_op jit(solution)/shard_map/ppermute | solution.py:420
  436.3 13.8 %collective-permute-start.45 = (bf16[2,128,1024]{2,1,0:T(8,128)(2,1)S(1)}, bf16[2,128,1024]{2,1,0:T(8,128)(2,1)S(1)}, u32[]{:S(2)}, u32[]{:S(2)}) collective-permute-start(bf16[2,128,1024]{2,1,0:T(8,128)(2,1)S(1)} %get-tuple-element.136), channel_id=1, source_target_pairs={{0,8},{4,12},{8,0},{12,4},{16,24},{20,28},{24,16},{28,20},{1,9},{5... | collective-permute-start | bytes 1572872 | tf_op jit(solution)/shard_map/ppermute | solution.py:420
  437.7 13.3 %collective-permute-start.40 = (bf16[2,32,4096]{2,1,0:T(8,128)(2,1)S(1)}, bf16[2,32,4096]{2,1,0:T(8,128)(2,1)S(1)}, u32[]{:S(2)}, u32[]{:S(2)}) collective-permute-start(bf16[2,32,4096]{2,1,0:T(8,128)(2,1)S(1)} %get-tuple-element.138), channel_id=1, source_target_pairs={{0,4},{4,0},{8,12},{12,8},{16,20},{20,16},{24,28},{28,24},{1,5},{5... | collective-permute-start | bytes 1572872 | tf_op jit(solution)/shard_map/ppermute | solution.py:420
  450.1 13.2 %collective-permute-start.46 = (bf16[128,1024]{1,0:T(8,128)(2,1)S(1)}, bf16[128,1024]{1,0:T(8,128)(2,1)S(1)}, u32[]{:S(2)}, u32[]{:S(2)}) collective-permute-start(bf16[128,1024]{1,0:T(8,128)(2,1)S(1)} %fusion.33), channel_id=1, source_target_pairs={{0,16},{4,20},{8,24},{12,28},{16,0},{20,4},{24,8},{28,12},{1,17},{... | collective-permute-start | bytes 786440 | tf_op jit(solution)/shard_map/ppermute | solution.py:420
  451.0 13.3 %collective-permute-start.41 = (bf16[32,4096]{1,0:T(8,128)(2,1)S(1)}, bf16[32,4096]{1,0:T(8,128)(2,1)S(1)}, u32[]{:S(2)}, u32[]{:S(2)}) collective-permute-start(bf16[32,4096]{1,0:T(8,128)(2,1)S(1)} %fusion.31), channel_id=1, source_target_pairs={{0,2},{1,3},{2,0},{3,1},{4,6},{5,7},{6,4},{7,5},{8,10},{9,11},{10,... | collective-permute-start | bytes 786440 | tf_op jit(solution)/shard_map/ppermute | solution.py:420
  (52 other events, 601.7 us)

commit v2 on v1

v2 whole, which is shorter than its diff:
```python
import jax
import jax.numpy as jnp
import numpy as np
from jax import lax
from jax.experimental import pallas as pl
from jax.experimental.pallas import tpu as pltpu
from jax.sharding import PartitionSpec as P

HEADS = 16
norm_eps = 1e-06
bf16 = jnp.bfloat16
f32 = jnp.float32
MIB = 1024 * 1024
DIGITS, BASE = 3, 11
CODE = DIGITS * BASE
HALF = 64


def dg(a, b, ca, cb):
    return lax.dot_general(a, b, (((ca,), (cb,)), ((), ())), preferred_element_type=f32)


def params(mib):
    return pltpu.CompilerParams(vmem_limit_bytes=mib * MIB)


def cost(flops, bytes_accessed, transcendentals=0):
    return pl.CostEstimate(
        flops=20 * flops, bytes_accessed=20 * bytes_accessed, transcendentals=transcendentals
    )


def core_parts(grad, chunk, core):
    rows, cols = grad.shape
    runs = grad.reshape(rows // (2 * chunk), 2, chunk, cols)
    even = runs[:, 0].reshape(rows // 2, cols)
    odd = runs[:, 1].reshape(rows // 2, cols)
    first = core == 0
    return jnp.where(first, odd, even), jnp.where(first, even, odd)


def put_parts(refs, grad, chunk, core):
    if len(refs) == 1:
        refs[0][...] = grad.astype(bf16)
    else:
        other, own = core_parts(grad, chunk, core)
        refs[0][...] = other.astype(bf16)
        refs[1][...] = own.astype(bf16)


def full_spec(rows, cols):
    return pl.BlockSpec((rows, cols), lambda i, *_: (0, 0), pipeline_mode=pl.Buffered(1))


def call(kernel, scalars, grid, ins, in_specs, outs, out_specs, scratch=(), aliases=None, est=None):
    return pl.pallas_call(
        kernel,
        grid_spec=pltpu.PrefetchScalarGridSpec(
            num_scalar_prefetch=1,
            grid=(grid,),
            in_specs=in_specs,
            out_specs=out_specs,
            scratch_shapes=list(scratch),
        ),
        out_shape=outs,
        input_output_aliases=aliases or {},
        compiler_params=params(60),
        cost_estimate=est,
    )(scalars, *ins)


def norm_parts(values):
    mean = jnp.mean(values, axis=-1, keepdims=True)
    centered = values - mean
    variance = jnp.mean(centered * centered, axis=-1, keepdims=True)
    rstd = lax.rsqrt(variance + norm_eps)
    return centered * rstd, rstd


def qkv_kernel(s, c0, c1, gain, shift, wq, wk, wv, bq, bv, *refs):
    x, nT, q, k, v, n_scr = refs[-6:]
    length = c0.shape[0]
    core = s[1]

    @pl.when(pl.program_id(0) == 0)
    def _():
        for chunk, at in ((c0, core), (c1, 1 - core)):
            rows = pl.ds(pl.multiple_of(at * length, length), length)
            values = chunk[...]
            x[rows, :] = values
            n, _ = norm_parts(values.astype(f32))
            n_scr[rows, :] = (n * gain[...] + shift[...]).astype(bf16)

    n = n_scr[...]
    block = wq.shape[1]
    q[...] = (dg(n, wq[...], 1, 0) + bq[...]).astype(bf16) * 0.125
    k[...] = dg(n, wk[...], 1, 0).astype(bf16)
    v[...] = (dg(n, wv[...], 1, 0) + bv[...]).astype(bf16)
    nT[...] = n_scr[:, pl.ds(pl.multiple_of(pl.program_id(0) * block, block), block)].T


def qkv(scalars, chunks, gain, shift, wq, wk, wv, bq, bv, before):
    length, width = chunks[0].shape
    total = 4 * length
    block = 256
    whole = full_spec(length, width)
    vec = full_spec(1, width)
    part = pl.BlockSpec((width, block), lambda i, s: (0, i))
    bias = pl.BlockSpec((1, block), lambda i, s: (0, i))
    wide = pl.BlockSpec((2 * length, width), lambda i, s: (s[0], 0), pipeline_mode=pl.Buffered(1))
    rows = pl.BlockSpec((2 * length, block), lambda i, s: (s[0], i))
    cols = pl.BlockSpec((block, 2 * length), lambda i, s: (i, s[0]))
    out = jax.ShapeDtypeStruct((total, width), bf16)
    outT = jax.ShapeDtypeStruct((width, total), bf16)
    return call(
        qkv_kernel,
        scalars,
        width // block,
        [*chunks, gain, shift, wq, wk, wv, bq, bv, *before],
        [whole, whole, vec, vec, part, part, part, bias, bias]
        + [pl.BlockSpec(memory_space=pl.ANY)] * len(before),
        [out, outT, out, out, out],
        [wide, cols, rows, rows, rows],
        [pltpu.VMEM((2 * length, width), bf16)],
        aliases={10 + n: n for n in range(len(before))},
        est=cost(2 * 2 * length * width * 3 * width, 20 * MIB),
    )


def pieces(value, row, base):
    hi = value.astype(bf16).astype(f32)
    mid = (value - hi).astype(bf16).astype(f32)
    low = value - hi - mid
    return jnp.where(
        row == CODE, hi, jnp.where(row == CODE + 1, mid, jnp.where(row == CODE + 2, low, base))
    )


def attend_kernel(q, k, v, fT, g, oT, olo, aux):
    total = k.shape[0]
    lane = lax.broadcasted_iota(jnp.int32, (total, 128), 1)
    row = lax.broadcasted_iota(jnp.int32, (HALF, total), 0)
    keys, codes, queries_code = k[...], g[...], fT[...]
    ones = jnp.ones((16, total), bf16)
    qT, vT = q[...].T, v[...].T

    def score(h):
        ka = jnp.where((lane < HALF) == (h == 0), keys, codes)
        qh = qT[h * HALF : (h + 1) * HALF, :]
        qa = jnp.concatenate([qh, queries_code] if h == 0 else [queries_code, qh], 0)
        s = dg(ka, qa, 1, 0)
        return s, jnp.max(s, axis=0, keepdims=True)

    def finish(h, s, top):
        head = slice(h * HALF, (h + 1) * HALF)
        va = jnp.concatenate([vT[head, :], ones], 0)
        p = jnp.exp(s - top).astype(bf16)
        mixed = dg(va, p, 1, 0)
        weight = mixed[HALF : HALF + 1]
        out = mixed[:HALF] / weight
        low = out.astype(bf16)
        oT[head, :] = low
        olo[head, :] = (out - low.astype(f32)).astype(bf16)
        aux[head, :] = pieces(
            -(top + jnp.log(weight)), row, queries_code.astype(f32)
        ).astype(bf16)

    first = score(0)
    second = score(1)
    finish(0, *first)
    finish(1, *second)


def attend(q, k, v, fT, g):
    total, width = q.shape
    tall = pl.BlockSpec((total, 128), lambda i: (0, i))
    pair = pl.BlockSpec((128, total), lambda i: (i, 0))
    return pl.pallas_call(
        attend_kernel,
        grid=(width // 128,),
        in_specs=[
            tall,
            tall,
            tall,
            pl.BlockSpec((HALF, total), lambda i: (0, 0)),
            pl.BlockSpec((total, 128), lambda i: (0, 0)),
        ],
        out_specs=[pair] * 3,
        out_shape=[jax.ShapeDtypeStruct((width, total), bf16)] * 3,
        compiler_params=params(60),
        cost_estimate=cost(16 * HEADS * total * total * 64, 12 * MIB, HEADS * total * total),
    )(q, k, v, fT, g)


def norm_back(n, rstd, grad, gain):
    gh = grad * gain
    mean = jnp.mean(gh, axis=-1, keepdims=True)
    tilt = jnp.mean(gh * n, axis=-1, keepdims=True)
    return rstd * (gh - mean - n * tilt)


def mlp_kernel(
    chunks, heads, cut, s, oT, x, wo, bo, gain, shift, wu, wd, bu, bd, *refs
):
    grads_in, outs = refs[:heads], refs[heads : 2 * heads]
    gbu, rg, bg, ggain, gshift, gb, *refs = refs[2 * heads :]
    step, steps = pl.program_id(0), pl.num_programs(0)
    per = (len(refs) - 6) // 3
    gwd, gwu0, gwu1 = refs[:per], refs[per : 2 * per], refs[2 * per : 3 * per]
    acc_o, acc_n, res, n2, di, oT_scr = refs[-6:]
    total = n2.shape[0]
    block = x.shape[0]
    after = steps - 2

    @pl.when(step < heads)
    def _():
        rows = pl.ds(pl.multiple_of(step * block, block), block)
        r = x[...].astype(f32) + dg(oT[...], wo[...], 0, 0) + bo[...]
        res[rows, :] = r
        acc_o[rows, :] = r + bd[...]
        n, _ = norm_parts(r)
        n2[rows, :] = (n * gain[...] + shift[...]).astype(bf16)
        oT_scr[:, rows] = oT[...]

    @pl.when(step == 0)
    def _():
        for j, ref in enumerate(grads_in):
            di[pl.ds(pl.multiple_of((s[2] ^ j) * block, block), block), :] = ref[...]

    @pl.when((step >= heads) & (step < after))
    def _():
        pre = dg(n2[...], wu[...], 1, 0) + bu[...]
        dact = dg(di[...], wd[...], 1, 1)
        cdf = 0.5 * (1.0 + lax.erf(pre * np.float32(np.sqrt(0.5))))
        pdf = jnp.exp(-0.5 * pre * pre) * np.float32(1 / np.sqrt(2 * np.pi))
        act = (pre * cdf).astype(bf16)
        acc_o[...] += dg(act, wd[...], 1, 0)
        hidden = (dact * (cdf + pre * pdf)).astype(bf16)
        new = dg(hidden, wu[...], 1, 1)

        @pl.when(step == heads)
        def _():
            acc_n[...] = new

        @pl.when(step > heads)
        def _():
            acc_n[...] += new

        down_grad = dg(act, di[...], 0, 0)
        if len(gwd) == 1:
            gwd[0][...] = down_grad.astype(bf16)
        else:
            rows, size = chunks
            width = down_grad.shape[1]
            for ref, part in zip(gwd, core_parts(down_grad, rows, s[1])):
                for at in range(0, part.shape[0], size):
                    device, place = at // rows, at % rows // size
                    ref[device * size : (device + 1) * size, place * width : (place + 1) * width] = (
                        part[at : at + size, :].astype(bf16)
                    )
        gbu[...] = jnp.sum(hidden.astype(f32), axis=0, keepdims=True)
        up_grad = dg(n2[...], hidden, 0, 0)

        @pl.when(step < heads + cut)
        def _():
            put_parts(gwu0, up_grad, chunks[1], s[1])

        @pl.when(step >= heads + cut)
        def _():
            put_parts(gwu1, up_grad, chunks[1], s[1])

    @pl.when(step == after)
    def _():
        for j, ref in enumerate(outs):
            rows = pl.ds(pl.multiple_of((s[2] ^ j) * block, block), block)
            ref[...] = acc_o[rows, :].astype(bf16)
        ggain[...] = jnp.zeros_like(ggain)
        gshift[...] = jnp.zeros_like(gshift)
        gb[...] = jnp.zeros_like(gb)

        @pl.loop(0, total // 256)
        def _(i):
            rows = pl.ds(pl.multiple_of(i * 256, 256), 256)
            n, rstd = norm_parts(res[rows, :])
            grad = acc_n[rows, :]
            ggain[...] += jnp.sum(grad * n, axis=0, keepdims=True)
            gshift[...] += jnp.sum(grad, axis=0, keepdims=True)
            resid = di[rows, :].astype(f32) + norm_back(n, rstd, grad, gain[...])
            rg[rows, :] = resid
            low = resid.astype(bf16)
            bg[rows, :] = low
            gb[...] += jnp.sum(low.astype(f32), axis=0, keepdims=True)

    @pl.when(step >= after)
    def _():
        half = bg.shape[1] // 2
        cols = pl.ds(pl.multiple_of((step - after) * half, half), half)
        put_parts(gwu1, dg(oT_scr[...], bg[:, cols], 1, 0), chunks[1], s[1])


def mlp(scalars, devices, cut, oT, x, wo, bo, gain, shift, di, wu, wd, bu, bd):
    total, width = x.shape
    hidden = wu.shape[1]
    rows_block, block = 256, 512
    heads = total // rows_block
    steps = hidden // block
    chunks = hidden // devices, width // devices
    parts = 2 if min(chunks) % 16 == 0 else 1
    down_shape = (width // 2, hidden) if parts == 2 else (hidden, width)
    full = full_spec(total, width)
    vec = full_spec(1, width)

    def early(i):
        return jnp.minimum(i, heads - 1)

    def late(i):
        return jnp.clip(i - heads, 0, steps - 1)

    tokens = pl.BlockSpec((rows_block, width), lambda i, s: (early(i), 0))
    up = pl.BlockSpec((width, block), lambda i, s: (0, late(i)))
    down = pl.BlockSpec((block, width), lambda i, s: (late(i), 0))
    bias = pl.BlockSpec((1, block), lambda i, s: (0, late(i)))
    row = jax.ShapeDtypeStruct((1, width), f32)
    got = call(
        lambda *refs: mlp_kernel(chunks, heads, cut, *refs),
        scalars,
        heads + steps + width // block,
        [oT, x, wo, bo, gain, shift, wu, wd, bu, bd, *di],
        [
            pl.BlockSpec((width, rows_block), lambda i, s: (0, early(i))),
            tokens,
            full_spec(width, width),
            vec,
            vec,
            vec,
            up,
            down,
            bias,
            vec,
        ]
        + [full_spec(rows_block, width)] * heads,
        [jax.ShapeDtypeStruct((rows_block, width), bf16)] * heads
        + [
            jax.ShapeDtypeStruct((1, hidden), f32),
            jax.ShapeDtypeStruct((total, width), f32),
            jax.ShapeDtypeStruct((total, width), bf16),
            row,
            row,
            row,
        ]
        + [jax.ShapeDtypeStruct(down_shape, bf16)] * parts
        + [jax.ShapeDtypeStruct((width // parts, cut * block), bf16)] * parts
        + [jax.ShapeDtypeStruct((width // parts, hidden - cut * block + width), bf16)] * parts,
        [full_spec(rows_block, width)] * heads
        + [bias, full, full, vec, vec, vec]
        + [pl.BlockSpec((down_shape[0] // steps, down_shape[1]), lambda i, s: (late(i), 0))] * parts
        + [
            pl.BlockSpec(
                (width // parts, block), lambda i, s: (0, jnp.clip(i - heads, 0, cut - 1))
            )
        ]
        * parts
        + [
            pl.BlockSpec(
                (width // parts, block), lambda i, s: (0, jnp.maximum(i - heads - cut, 0))
            )
        ]
        * parts,
        [
            pltpu.VMEM((total, width), f32),
            pltpu.VMEM((total, width), f32),
            pltpu.VMEM((total, width), f32),
            pltpu.VMEM((total, width), bf16),
            pltpu.VMEM((total, width), bf16),
            pltpu.VMEM((width, total), bf16),
        ],
        est=cost(2 * total * width * (6 * hidden + 2 * width), 70 * MIB, 2 * total * hidden),
    )
    outs, got = got[:heads], got[heads:]
    return outs, got[:6], got[6 : 6 + parts], got[6 + parts : 6 + 2 * parts], got[6 + 2 * parts :]


def attend_back_kernel(chunk, s, q, k, v, w, bg, oT, olo, aux, g, nT, *refs):
    dqT, dkT, dvT, bias, *grads = refs
    total = k.shape[0]
    lane = lax.broadcasted_iota(jnp.int32, (total, 128), 1)
    row = lax.broadcasted_iota(jnp.int32, (HALF, total), 0)
    keys, values, codes = k[...], v[...], g[...]
    qT, kT = q[...].T, keys.T
    doT = dg(w[...], bg[...], 1, 1).astype(bf16)
    parts = [[], [], []]
    for h in range(2):
        head = slice(h * HALF, (h + 1) * HALF)
        mine = (lane < HALF) == (h == 0)
        ka = jnp.where(mine, keys, codes)
        va = jnp.where(mine, values, codes)
        doh, qh, ax = doT[head, :], qT[head, :], aux[head, :]
        full = oT[head, :].astype(f32) + olo[head, :].astype(f32)
        delta = -jnp.sum(doh.astype(f32) * full, axis=0, keepdims=True)
        dx = pieces(delta, row, 0.0).astype(bf16)
        qa = jnp.concatenate([qh, ax] if h == 0 else [ax, qh], 0)
        doa = jnp.concatenate([doh, dx] if h == 0 else [dx, doh], 0)
        scores = dg(ka, qa, 1, 0)
        dp = dg(va, doa, 1, 0)
        p = jnp.exp(scores)
        low = p.astype(bf16)
        ds = (p * dp).astype(bf16)
        parts[1].append(dg(qh, ds, 1, 1).astype(bf16))
        parts[2].append(dg(doh, low, 1, 1).astype(bf16))
        parts[0].append((dg(kT[head, :], ds, 1, 0) * 0.125).astype(bf16))
    new = jnp.concatenate([p for pair in parts for p in pair], 0)
    for n, ref in enumerate((dqT, dkT, dvT)):
        ref[...] = new[128 * n : 128 * (n + 1)]
    put_parts(grads, dg(nT[...], new, 1, 1), chunk, s[1])
    bias[...] = dg(jnp.ones((8, total), bf16), new, 1, 1)[:1]


def attend_back(scalars, devices, first, pairs, q, k, v, w, bg, oT, olo, aux, g, nT, before):
    total, width = q.shape
    chunk = width // devices
    parts = 2 if chunk % 16 == 0 else 1
    pair = pl.BlockSpec((128, total), lambda i, s: (i + first, 0))
    tall = pl.BlockSpec((total, 128), lambda i, s: (0, i + first))
    done = pl.BlockSpec((128, total), lambda i, s: (i, 0))
    outs = call(
        lambda *refs: attend_back_kernel(chunk, *refs[:11], *refs[11 + len(before) :]),
        scalars,
        pairs,
        [q, k, v, w, bg, oT, olo, aux, g, nT, *before],
        [tall, tall, tall, pl.BlockSpec((128, width), lambda i, s: (i + first, 0))]
        + [full_spec(total, width), pair, pair, pair]
        + [full_spec(total, 128), full_spec(width, total)]
        + [pl.BlockSpec(memory_space=pl.ANY)] * len(before),
        [jax.ShapeDtypeStruct((128 * pairs, total), bf16)] * 3
        + [jax.ShapeDtypeStruct((1, 384 * pairs), f32)]
        + [jax.ShapeDtypeStruct((width // parts, 3 * width), bf16)] * parts,
        [done] * 3
        + [pl.BlockSpec((1, 384), lambda i, s: (0, i))]
        + [pl.BlockSpec((width // parts, 384), lambda i, s: (0, i + first))] * parts,
        aliases={11 + n: 4 + n for n in range(len(before))},
        est=cost(pairs * 100 * 2 * total * total * 64, pairs * 3 * MIB, pairs * 2 * total * total),
    )
    return outs[:3], outs[3], list(outs[4:])


def token_grad_kernel(count, groups, s, *refs):
    grads = refs[:count]
    wq, wk, wv, x, rg, gain, *more = refs[count:-6]
    outs, eight, acc = refs[-6:-2], refs[-2], refs[-1]
    biases, rows = more[:groups], more[groups:]
    step = pl.program_id(0)

    @pl.when(step == 0)
    def _():
        eight[...] = jnp.zeros_like(eight)
        acc[...] = jnp.zeros_like(acc)
        for n, ref in enumerate(rows):
            eight[4 + n : 5 + n, :] = ref[...]
        at = 0
        for ref in biases:
            for n in range(ref.shape[1] // 384):
                eight[2:3, at : at + 128] = ref[:, 384 * n : 384 * n + 128]
                eight[3:4, at : at + 128] = ref[:, 384 * n + 256 : 384 * n + 384]
                at += 128

    grad = acc[...]
    new = 0.0
    for n, w in enumerate((wq, wk, wv)):
        new = new + dg(jnp.concatenate([g[...] for g in grads[n::3]], 0), w[...], 0, 1)
    n, rstd = norm_parts(x[...].astype(f32))
    eight[0:1, :] += jnp.sum(grad * n, axis=0, keepdims=True)
    eight[1:2, :] += jnp.sum(grad, axis=0, keepdims=True)
    done = (rg[...] + norm_back(n, rstd, grad, gain[...])).astype(bf16)
    for j, out in enumerate(outs):

        @pl.when((step - 1) == (s[2] ^ j))
        def _(out=out):
            out[...] = done

    acc[...] = new


def token_grad(scalars, grads, wq, wk, wv, x, rg, gain, biases, rows):
    total, width = x.shape
    block = 256
    steps = total // block
    grads = [g for triple in grads for g in triple]

    def now(i):
        return jnp.minimum(i, steps - 1)

    def past(i):
        return jnp.maximum(i - 1, 0)

    tokens = pl.BlockSpec((block, width), lambda i, s: (past(i), 0))
    vec = full_spec(1, width)
    return call(
        lambda *refs: token_grad_kernel(len(grads), len(biases), *refs),
        scalars,
        steps + 1,
        [*grads, wq, wk, wv, x, rg, gain, *biases, *rows],
        [pl.BlockSpec((g.shape[0], block), lambda i, s: (0, now(i))) for g in grads]
        + [full_spec(width, width)] * 3
        + [tokens, tokens, vec]
        + [full_spec(*b.shape) for b in biases]
        + [vec] * len(rows),
        [jax.ShapeDtypeStruct((block, width), bf16)] * steps
        + [jax.ShapeDtypeStruct((8, width), f32)],
        [full_spec(block, width)] * steps + [full_spec(8, width)],
        [pltpu.VMEM((block, width), f32)],
        est=cost(6 * total * width * width, 24 * MIB),
    )


def gather_kernel(s, *refs):
    parts, (out, sems) = refs[:-2], refs[-2:]
    copies = [
        pltpu.make_async_copy(ref, out.at[s[2] ^ j], sems.at[j]) for j, ref in enumerate(parts)
    ]
    for copy in copies:
        copy.start()
    for copy in copies:
        copy.wait()


def gather(scalars, parts):
    return call(
        gather_kernel,
        scalars,
        1,
        parts,
        [full_spec(*part.shape) for part in parts],
        jax.ShapeDtypeStruct((len(parts), *parts[0].shape), parts[0].dtype),
        pl.BlockSpec(memory_space=pl.ANY),
        [pltpu.SemaphoreType.DMA((len(parts),))],
    )


AXES = ("rows", "seq")


def swap(values, mask, devices):
    return lax.ppermute(values, AXES, [(d, d ^ mask) for d in range(devices)])


def add_kernel(jobs, arrays, s, *refs):
    ins, outs = refs[:arrays], refs[arrays : arrays + len(jobs)]
    refs = list(refs[arrays + len(jobs) :])
    sem_in, sem_out = refs[-2:]
    loads, stores, at, count = [], [], 0, 0
    for job, (free, segments) in enumerate(jobs):
        result = refs[at]
        at += 1
        places = []
        for width, terms in segments:
            places.append((width, refs[at : at + len(terms)]))
            at += len(terms)
        for piece in range(2 if free else 1):
            copies = []
            for (width, terms), (_, buffers) in zip(segments, places):
                for buffer, (array, index, column) in zip(buffers, terms):
                    where, first = [], True
                    for entry in index:
                        if entry is None:
                            where.append(piece if first else slice(None))
                            first = False
                        else:
                            where.append(s[entry])
                    where += [slice(None), pl.ds(column, width)]
                    copies.append(
                        pltpu.make_async_copy(
                            ins[array].at[tuple(where)],
                            buffer.at[piece] if free else buffer,
                            sem_in.at[count],
                        )
                    )
                    copies[-1].start()
                    count += 1
            loads.append((job, piece, free, places, result, copies))
    for spot, (job, piece, free, places, result, copies) in enumerate(loads):
        for copy in copies:
            copy.wait()
        for n in range(2 ** max(free - 1, 0)):
            here = ((piece,) if free else ()) + tuple(n >> b & 1 for b in range(free - 1))
            column = 0
            for width, buffers in places:
                total = sum(buffer[here].astype(f32) for buffer in buffers)
                result[here + (slice(None), slice(column, column + width))] = total.astype(
                    result.dtype
                )
                column += width
        stores.append(
            pltpu.make_async_copy(
                result.at[piece] if free else result,
                outs[job].at[piece] if free else outs[job],
                sem_out.at[spot],
            )
        )
        stores[-1].start()
    for copy in stores:
        copy.wait()


def add_all(wanted):
    arrays, entries, jobs, scratch, outs, shapes = [], [], [], [], [], []
    copies = pieces_out = 0
    for dtype, chunk, free, segments in wanted:
        shape = (2,) * free + (chunk, sum(width for width, _ in segments))
        scratch.append(pltpu.VMEM(shape, dtype))
        outs.append(jax.ShapeDtypeStruct(shape, dtype))
        pieces_out += 2 if free else 1
        listed = []
        for width, terms in segments:
            row = []
            for array, index, column in terms:
                found = [n for n, other in enumerate(arrays) if other is array]
                if not found:
                    arrays.append(array)
                    shapes.append((2,) * len(index) + (chunk, array.shape[-1]))
                where = []
                for value in index:
                    where.append(None if value is None else len(entries))
                    if value is not None:
                        entries.append(value)
                row.append((found[0] if found else len(arrays) - 1, where, column))
                scratch.append(pltpu.VMEM((2,) * free + (chunk, width), array.dtype))
                copies += 2 if free else 1
            listed.append((width, row))
        jobs.append((free, listed))
    anyspec = pl.BlockSpec(memory_space=pl.ANY)
    got = call(
        lambda *refs: add_kernel(jobs, len(arrays), *refs),
        jnp.stack([jnp.int32(e) for e in entries]),
        1,
        [array.reshape(shape) for array, shape in zip(arrays, shapes)],
        [anyspec] * len(arrays),
        outs,
        [anyspec] * len(outs),
        scratch + [pltpu.SemaphoreType.DMA((copies,)), pltpu.SemaphoreType.DMA((pieces_out,))],
    )
    return [values.reshape(-1, values.shape[-1]) for values in got]


class Sum:
    def __init__(self, devices, spots, segments, order):
        self.devices, self.spots, self.order = devices, list(spots), list(order)
        self.me = lax.axis_index(AXES)
        self.sending, self.coming, self.taken, self.total = [], [], [], None
        if segments:
            self.chunk = segments[0][0][0].shape[0] >> len(self.spots)
        self.segments = [
            (width, [(array, list(self.spots), column) for array in arrays])
            for arrays, column, width in segments
        ]

    def merged(self, other, order):
        new = Sum(self.devices, self.spots, [], order)
        new.chunk, new.taken = self.chunk, list(self.taken)
        new.segments = self.segments + other.segments
        return new

    def wanted(self, mask, dtype, segments):
        bits = {bit: ((self.me ^ mask) >> bit) & 1 for bit in self.taken}
        listed = [
            (width, [(v, [bits.get(bit) for bit in spots], column) for v, spots, column in terms])
            for width, terms in segments
        ]
        return (dtype, self.chunk, len(self.spots), listed)

    def masks(self):
        step = self.order.pop(0)
        bits = step if isinstance(step, tuple) else (step,)
        masks = [0]
        for bit in bits:
            masks += [m | 1 << bit for m in masks]
        self.taken += bits
        for bit in bits:
            self.spots.remove(bit)
        return masks[1:]

    def start(self):
        self.coming += [swap(v, mask, self.devices) for mask, v in self.sending]
        self.sending = []

    def arrive(self, coming):
        column = 0
        for width, terms in self.segments:
            terms += [(v, list(self.spots), column) for v in coming]
            column += width
        self.coming = []


def prepare(sums):
    jobs = []
    for t in sums:
        if t.order:
            jobs += [(t, mask, bf16, t.segments) for mask in t.masks()]
        elif t.total is None:
            jobs += [(t, 0, f32, [segment]) for segment in t.segments]
            t.total = []
    if not jobs:
        return
    got = add_all([t.wanted(mask, dtype, segments) for t, mask, dtype, segments in jobs])
    for (t, mask, dtype, _), values in zip(jobs, got):
        if dtype == f32:
            t.total.append(values)
        else:
            t.sending.append((mask, values))


def together(*groups):
    flat = lax.optimization_barrier(tuple(v for group in groups for v in group))
    out, start = [], 0
    for group in groups:
        out.append(list(flat[start : start + len(group)]))
        start += len(group)
    return out


def arrive(sums, carry):
    got = together(carry, *[t.coming for t in sums])
    for t, coming in zip(sums, got[1:]):
        t.arrive(coming)
    return got[0]


def leave(sums, carry):
    prepare(sums)
    got = together(carry, *[[v for _, v in t.sending] for t in sums])
    for t, sending in zip(sums, got[1:]):
        t.sending = [(mask, v) for (mask, _), v in zip(t.sending, sending)]
        t.start()
    return got[0]


def on_device(
    tokens,
    segment_ids,
    grad_out,
    norm1_gain,
    norm1_shift,
    w_query,
    b_query,
    w_key,
    w_value,
    b_value,
    w_out,
    b_out,
    norm2_gain,
    norm2_shift,
    w_up,
    b_up,
    w_down,
    b_down,
):
    row_count, local_len, width = tokens.shape
    full_len = segment_ids.shape[1]
    hidden = w_up.shape[1]
    seq, rows = lax.axis_size("seq"), lax.axis_size("rows")
    devices = rows * seq
    me = lax.axis_index("seq")
    core, pair = me % 2, me // 2
    assert row_count == seq == 4 and local_len * seq == full_len

    def vec(v):
        return v.reshape(1, -1)

    def scalars(first):
        return jnp.stack([jnp.int32(first), jnp.int32(core), jnp.int32(me)])

    def exchange(parts):
        return [parts[0]] + [swap(parts[j], j, devices) for j in range(1, seq)]

    plain = scalars(0)
    chunks = [lax.dynamic_index_in_dim(tokens, me ^ j, 0, keepdims=False) for j in range(seq)]
    chunks = exchange(chunks)
    norm1 = (vec(norm1_gain), vec(norm1_shift))
    weights = (w_query, w_key, w_value, vec(b_query), vec(b_value))

    ids = lax.dynamic_index_in_dim(segment_ids, me, 0, keepdims=False)
    digits = jnp.stack([(ids // BASE**n) % BASE for n in range(DIGITS)], 1)
    hot = (digits[:, :, None] == jnp.arange(BASE)[None, None, :]).reshape(full_len, CODE)
    hot = hot.astype(f32)
    rest = jnp.zeros((full_len, HALF - CODE), f32)
    query_code = jnp.concatenate([hot, rest], 1).astype(bf16).T
    key_code = jnp.concatenate([-1e30 * (1.0 - hot), rest.at[:, :3].set(1.0)], 1).astype(bf16)
    key_code = jnp.concatenate([key_code, key_code], 1)

    local_ids = lax.dynamic_slice_in_dim(segment_ids, me * local_len, local_len, 1)
    is_image = (local_ids != full_len).astype(bf16)[:, :, None]
    out_grad = grad_out * is_image
    grad_b_down = jnp.sum(out_grad.astype(f32), axis=(0, 1))

    before = qkv(scalars(pair), chunks[:2], *norm1, *weights, ())
    before = list(before)
    [before[0]], [out_grad] = together([before[0]], [out_grad])
    others = chunks[2:]
    down_in = exchange([lax.dynamic_index_in_dim(out_grad, me ^ j, 0, keepdims=False) for j in range(seq)])
    x, normedT, q, k, v = qkv(scalars(1 - pair), others, *norm1, *weights, before)
    oT, olo, aux = attend(q, k, v, query_code, key_code)
    nbits = devices.bit_length() - 1
    far = tuple(range(3, nbits))
    every = list(range(nbits - 1, -1, -1))
    block_out, (grad_b_up, rg, bg, gain2, shift2, bias_out), grad_down, grad_up0, grad_up1 = mlp(
        plain,
        devices,
        4,
        oT,
        x,
        w_out,
        vec(b_out),
        vec(norm2_gain),
        vec(norm2_shift),
        down_in,
        w_up,
        w_down,
        vec(b_up),
        vec(b_down),
    )
    biases, grads = [], []

    def backward(first, pairs, bg, before):
        got, bias, parts = attend_back(
            plain, devices, first, pairs, q, k, v, w_out, bg, oT, olo, aux, key_code, normedT, before
        )
        grads.append(got)
        biases.append(bias)
        return parts

    split = len(grad_down) == 2 and nbits == 5
    spots = every[:-1]

    def on_chip(pairs, carry):
        sends = [pair_[0] for pair_ in pairs]
        carry, sends = together(carry, sends)
        return carry, [swap(v, 1, devices) for v in sends]

    made = [grad_down, grad_up0, grad_up1]
    block_out = list(block_out)
    if split:
        [bg], came = on_chip(made, [bg])
    block_out[2:] = [swap(block_out[j], j, devices) for j in range(2, seq)]
    parts = backward(0, 2, bg, ())
    if split:
        (parts[0], bg, *block_out[2:]), came = together([parts[0], bg, *block_out[2:]], came)
        down, up0, up1 = ([keep, other] for (_, keep), other in zip(made, came))
        sum_a = Sum(devices, spots, [(down, 0, 3328)], [2, 1])
        sum_b = Sum(devices, spots, [(down, 3328, 768), (up1, 512, 2560)], [1, 2])
        sum_c = Sum(devices, spots, [(up0, 0, 2048), (up1, 0, 512)], [3, 4, 2, 1])
        sums = [sum_a, sum_b, sum_c]
        parts[0], bg = leave(sums, [parts[0], bg])
    block_out[1] = swap(block_out[1], 1, devices)
    parts = backward(2, 4, bg, parts)
    if split:
        parts[0], bg, *block_out = arrive(sums, [parts[0], bg, *block_out])
        parts[0], bg = leave(sums, [parts[0], bg])
    parts = backward(6, 2, bg, parts)
    gain = vec(norm1_gain)
    if split:
        parts[0], gain = arrive(sums, [parts[0], gain])
        [gain], came = on_chip([parts], [gain])
        sum_ab = sum_a.merged(sum_b, [3, 4])
        sums = [sum_ab, sum_c]
        [gain] = leave(sums, [gain])
        [gain], came = together([gain], came)
        ours = [parts[1], *came]
        cols = parts[1].shape[1] // 2
        sum_d = Sum(devices, spots, [(ours, 0, cols)], [2, 1])
        sum_e = Sum(devices, spots, [(ours, cols, cols)], [1, 2])
        [gain] = leave([sum_d, sum_e], [gain])
        sums += [sum_d, sum_e]
    *token, eight = token_grad(
        plain,
        grads,
        w_query,
        w_key,
        w_value,
        x,
        rg,
        gain,
        biases,
        [bias_out, gain2, shift2, vec(grad_b_down)],
    )
    if split:
        eight, *token = arrive(sums, [eight, *token])
        [eight] = leave(sums, [eight])
    token = exchange(token)
    eight = jnp.transpose(eight.reshape(8, devices, -1), (1, 0, 2)).reshape(devices, -1)
    vectors = jnp.concatenate([eight, grad_b_up.reshape(devices, -1)], 1)
    vectors = lax.all_to_all(vectors, AXES, 0, 0, tiled=True)
    own = width // devices
    if split:
        vectors, *token = arrive(sums, [vectors, *token])
        sum_in = sum_d.merged(sum_e, [far])
        [vectors] = leave([sum_in, sum_ab, sum_c], [vectors])
        [vectors] = arrive([sum_in], [vectors])
        leave([sum_in], [])
        down0, down1, up1 = sum_ab.total
        up0, up_mid = sum_c.total
        grad_w_down = jnp.concatenate([down0, down1], 1).reshape(own, -1, width)
        grad_w_down = jnp.transpose(grad_w_down, (1, 0, 2)).reshape(-1, width)
        at = up1.shape[1] - width
        grad_w_up = jnp.concatenate([up0, up_mid, up1[:, :at]], 1)
        grad_w_out = up1[:, at:]
        qkv_sums = jnp.concatenate(sum_in.total, 1)
    else:

        def over_all(values):
            return lax.psum_scatter(values.astype(f32), AXES, scatter_dimension=0, tiled=True)

        grad_w_down, up0, up1, qkv_sums = (over_all(pair_[0]) for pair_ in (*made, parts))
        grad_w_up = jnp.concatenate([up0, up1[:, : hidden - up0.shape[1]]], 1)
        grad_w_out = up1[:, hidden - up0.shape[1] :]
    vectors = jnp.sum(vectors, 0)
    grad_tokens = gather(plain, token)
    block_out = gather(plain, block_out)
    qkv_sums = qkv_sums.reshape(own, width // 128, 3, 128)
    grad_w_query, grad_w_key, grad_w_value = (
        qkv_sums[:, :, n].reshape(width // devices, width) for n in range(3)
    )
    parts, start = [], 0
    for size in [width] * 8 + [hidden]:
        parts.append(vectors[start : start + size // devices])
        start += size // devices
    gain1, shift1, bq, bv, bo, gain2, shift2, bd, bu = parts
    return (
        block_out,
        grad_tokens,
        gain1,
        shift1,
        grad_w_query,
        bq,
        grad_w_key,
        grad_w_value,
        bv,
        grad_w_out,
        bo,
        gain2,
        shift2,
        grad_w_up,
        bu,
        grad_w_down,
        bd,
    )


def solution(mesh):
    tokens = P("rows", "seq", None)
    spread = P(("rows", "seq"))
    spread2 = P(("rows", "seq"), None)
    return jax.shard_map(
        on_device,
        mesh=mesh,
        in_specs=(tokens, P("rows", None), tokens) + (P(),) * 15,
        out_specs=(
            tokens,
            tokens,
            spread,
            spread,
            spread2,
            spread,
            spread2,
            spread2,
            spread,
            spread2,
            spread,
            spread,
            spread,
            spread2,
            spread,
            spread2,
            spread,
        ),
        check_vma=False,
    )
```

time: 474 us -> 376 us (0.79)
  the two profiles are of different devices: /device:TPU:0 before, /device:TPU:16 now
where the time goes in v2:
time: 376 us; the launch traced here: 369 us
  Pallas kernels  258 us (69%)
  waiting for transfers between devices  41.6 us (11%)
  starting transfers between devices  34.4 us (9%)
  local copies, waits for them, and re-layouts  22.2 us (6%)
  other arithmetic  10.5 us (3%)
    pallas_call x16, Pallas kernels, call(): pl.pallas_call(kernel, grid_spec=pltpu.PrefetchScalarGridSpec(num_scalar_...  233 us
    ppermute x33, waiting for transfers between devices, swap(): return lax.ppermute(values, AXES, [(d, d ^ mask) for d in range(devices)])  32.1 us
    ppermute x33, starting transfers between devices, swap(): return lax.ppermute(values, AXES, [(d, d ^ mask) for d in range(devices)])  29.3 us
    pallas_call x1, Pallas kernels, attend(): pl.pallas_call(attend_kernel, grid=(width // 128,), in_specs=[tall, tall,...  24.8 us
    all_to_all x1, waiting for transfers between devices, on_device(): vectors = lax.all_to_all(vectors, AXES, 0, 0, tiled=True)  9.51 us
  transfers between devices with their start and end apart: 34, of which 9 were waited for; matrix products, arithmetic and copies ran while one was open for 5% of the time, Pallas kernels for 43%

profile of v2, /device:TPU:16, one launch (start us, length us, event | category | flops | bytes accessed | tf_op | source)
XLA Modules:
  0.0 368.7 jit_solution(1592656056926282722)
XLA Ops:
  0.7 2.5 dynamic-slice_bitcast_fusion.4
  3.2 1.6 collective-permute-start.1
  11.7 2.7 convert_reduce_fusion
  14.4 9.2 %shard_map.305 = (bf16[1024,1024]{1,0:T(8,128)(2,1)}, bf16[1024,1024]{1,0:T(8,128)(2,1)}, bf16[1024,1024]{1,0:T(8,128)(2,1)}, bf16[1024,1024]{1,0:T(8,128)(2,1)}, bf16[1024,1024]{1,0:T(8,128)(2,1)}) custom-call(s32[3]{0:T(128)} %add_add_fusion.2.s, bf16[256,1024]{1,0:T(8,128)(2,1)} %get-tuple-element.351.c0, bf16[256,1024]{1,0:T(8,128)(2,1)} %collective-permute-done.2.c1, ...), custom_call_target="tpu_custom_call" | custom-call | flops 64424509440 | bytes 419430400 | tf_op jit(solution)/shard_map/pallas_call | solution.py:56
  23.6 1.4 dynamic-slice_bitcast_fusion
  26.9 2.3 collective-permute-done.c0
  29.1 9.3 %shard_map.306 = (bf16[1024,1024]{1,0:T(8,128)(2,1)}, bf16[1024,1024]{1,0:T(8,128)(2,1)}, bf16[1024,1024]{1,0:T(8,128)(2,1)}, bf16[1024,1024]{1,0:T(8,128)(2,1)}, bf16[1024,1024]{1,0:T(8,128)(2,1)}) custom-call(s32[3]{0:T(128)} %get-tuple-element.364.s, ...), custom_call_target="tpu_custom_call", output_to_operand_aliasing={{0}: (10, {}), {1}: (11, {}), {2}: (12, {}), {3}: (13, {}),... | custom-call | flops 64424509440 | bytes 419430400 | tf_op jit(solution)/shard_map/pallas_call | solution.py:56
  38.4 24.8 %shard_map.307 = (bf16[1024,1024]{1,0:T(8,128)(2,1)}, bf16[1024,1024]{1,0:T(8,128)(2,1)}, bf16[1024,1024]{1,0:T(8,128)(2,1)}) custom-call(bf16[1024,1024]{1,0:T(8,128)(2,1)} %get-tuple-element.189.q.refs_1_, bf16[1024,1024]{1,0:T(8,128)(2,1)} %get-tuple-element.190.k.refs_2_, bf16[1024,1024]{1,0:T(8,128)(2,1)} %get-tuple-element.191.v.refs_3_, ...), custom_call_target="tpu_custom_call" | custom-call | flops 343597383680 | bytes 251658240 | tf_op jit(solution)/shard_map/pallas_call | solution.py:178
  63.3 81.2 %shard_map.308 = (bf16[256,1024]{1,0:T(8,128)(2,1)}, bf16[256,1024]{1,0:T(8,128)(2,1)}, bf16[256,1024]{1,0:T(8,128)(2,1)}, bf16[256,1024]{1,0:T(8,128)(2,1)}, f3...) custom-call(s32[3]{0:T(128)} %get-tuple-element.363.refs_0_.s, ...), custom_call_target="tpu_custom_call" | custom-call | flops 1116691496960 | bytes 1468006400 | tf_op jit(solution)/shard_map/pallas_call | solution.py:56
  144.5 1.6 collective-permute-start.6
  147.2 20.3 %shard_map.309 = (bf16[256,1024]{1,0:T(8,128)(2,1)}, bf16[256,1024]{1,0:T(8,128)(2,1)}, bf16[256,1024]{1,0:T(8,128)(2,1)}, f32[1,768]{1,0:T(1,128)}, bf16[512,30...) custom-call(s32[3]{0:T(128)} %get-tuple-element.363.refs_0_.s, bf16[1024,1024]{1,0:T(8,128)(2,1)} %get-tuple-element.189.q.refs_1_, ...), custom_call_target="tpu_custom_call" | custom-call | flops 536870912000 | bytes 125829120 | tf_op jit(solution)/shard_map/pallas_call | solution.py:56
  168.1 6.5 %shard_map.310 = (bf16[2,2,2,32,3328]{4,3,2,1,0:T(8,128)(2,1)}, bf16[2,2,2,32,3328]{4,3,2,1,0:T(8,128)(2,1)}, bf16[2,2,2,32,2560]{4,3,2,1,0:T(8,128)(2,1)}) custom-call(s32[10]{0:T(128)} %stack.89.refs_0_, bf16[2,2,2,2,32,4096]{5,4,3,2,1,0:T(8,128)(2,1)} %bitcast.141, bf16[2,2,2,2,32,4096]{5,4,3,2,1,0:T(8,128)(2,1)} %bitcast.31.refs_2_.refs_8_, ...), custom_call_target="tpu_custom_call" | custom-call | tf_op jit(solution)/shard_map/pallas_call | solution.py:56
  174.5 1.6 collective-permute-start.14
  176.2 1.5 collective-permute-start.12
  177.7 1.1 collective-permute-start.13
  178.8 35.0 %shard_map.311 = (bf16[512,1024]{1,0:T(8,128)(2,1)}, bf16[512,1024]{1,0:T(8,128)(2,1)}, bf16[512,1024]{1,0:T(8,128)(2,1)}, f32[1,1536]{1,0:T(1,128)}, bf16[512,3...) custom-call(s32[3]{0:T(128)} %get-tuple-element.363.refs_0_.s, ...), custom_call_target="tpu_custom_call", output_to_operand_aliasing={{4}: (11, {}), {5}: (12, {})} | custom-call | flops 1073741824000 | bytes 251658240 | tf_op jit(solution)/shard_map/pallas_call | solution.py:56
  213.8 2.4 collective-permute-done.12
  216.1 1.2 collective-permute-done.13
  217.3 5.3 %shard_map.313 = (bf16[2,2,32,3328]{3,2,1,0:T(8,128)(2,1)}, bf16[2,2,32,3328]{3,2,1,0:T(8,128)(2,1)}, bf16[2,2,32,2560]{3,2,1,0:T(8,128)(2,1)}) custom-call(s32[25]{0:T(128)} %stack.94.refs_0_, bf16[2,2,2,2,32,4096]{5,4,3,2,1,0:T(8,128)(2,1)} %bitcast.142, bf16[2,2,2,2,32,4096]{5,4,3,2,1,0:T(8,128)(2,1)} %bitcast.31.refs_2_.refs_8_, ...), custom_call_target="tpu_custom_call" | custom-call | tf_op jit(solution)/shard_map/pallas_call | solution.py:56
  223.0 1.5 collective-permute-start.15
  225.1 19.9 %shard_map.314 = (bf16[256,1024]{1,0:T(8,128)(2,1)}, bf16[256,1024]{1,0:T(8,128)(2,1)}, bf16[256,1024]{1,0:T(8,128)(2,1)}, f32[1,768]{1,0:T(1,128)}, bf16[512,30...) custom-call(s32[3]{0:T(128)} %get-tuple-element.363.refs_0_.s, ...), custom_call_target="tpu_custom_call", output_to_operand_aliasing={{4}: (11, {}), {5}: (12, {})} | custom-call | flops 536870912000 | bytes 125829120 | tf_op jit(solution)/shard_map/pallas_call | solution.py:56
  244.9 5.9 %collective-permute-done.17 = bf16[128,2560]{1,0:T(8,128)(2,1)} collective-permute-done((bf16[128,2560]{1,0:T(8,128)(2,1)}, bf16[128,2560]{1,0:T(8,128)(2,1)}, u32[]{:S(2)}, u32[]{:S(2)}) %collective-permute-start.17) | collective-permute-done | bytes 655392 | tf_op jit(solution)/shard_map/ppermute | solution.py:543
  252.8 4.2 %shard_map.315 = (bf16[2,32,6656]{2,1,0:T(8,128)(2,1)}, bf16[2,32,2560]{2,1,0:T(8,128)(2,1)}) custom-call(s32[45]{0:T(128)} %stack.99.refs_0_, bf16[2,2,2,2,32,4096]{5,4,3,2,1,0:T(8,128)(2,1)} %bitcast.143, bf16[2,2,2,2,32,4096]{5,4,3,2,1,0:T(8,128)(2,1)} %bitcast.31.refs_2_.refs_8_, bf16[2,2,2,32,3328]{4,3,2,1,0:T(8,128)(2,1)} %bitcast.43.refs_3_.refs_9_, ...), custom_call_target="tpu_custom_call" | custom-call | tf_op jit(solution)/shard_map/pallas_call | solution.py:56
  257.7 3.5 collective-permute-start.19
  261.2 1.6 copy-done
  262.9 3.4 shard_map.316
  266.3 1.5 collective-permute-start.21
  267.8 1.9 collective-permute-start.22
  269.7 19.2 %shard_map.317 = (bf16[256,1024]{1,0:T(8,128)(2,1)}, bf16[256,1024]{1,0:T(8,128)(2,1)}, bf16[256,1024]{1,0:T(8,128)(2,1)}, bf16[256,1024]{1,0:T(8,128)(2,1)}, f32[8,1024]{1,0:T(8,128)}) custom-call(s32[3]{0:T(128)} %get-tuple-element.363.refs_0_.s, bf16[256,1024]{1,0:T(8,128)(2,1)} %get-tuple-element.235.refs_1_, ...), custom_call_target="tpu_custom_call" | custom-call | flops 128849018880 | bytes 503316480 | tf_op jit(solution)/shard_map/pallas_call | solution.py:56
  290.3 4.6 %shard_map.318 = (bf16[32,6656]{1,0:T(8,128)(2,1)}, bf16[32,2560]{1,0:T(8,128)(2,1)}, bf16[2,2,32,1536]{3,2,1,0:T(8,128)(2,1)}, bf16[2,2,32,1536]{3,2,1,0:T(8,128)(2,1)}) custom-call(s32[80]{0:T(128)} %stack.105.refs_0_, bf16[2,2,2,2,32,4096]{5,4,3,2,1,0:T(8,128)(2,1)} %bitcast.144, bf16[2,2,2,2,32,4096]{5,4,3,2,1,0:T(8,128)(2,1)} %bitcast.31.refs_2_.refs_8_, ...), custom_call_target="tpu_custom_call" | custom-call | tf_op jit(solution)/shard_map/pallas_call | solution.py:56
  295.0 1.9 collective-permute-start.27
  297.1 1.7 collective-permute-start.25
  298.8 11.9 %collective-permute-done.27.refs_22_ = bf16[32,2560]{1,0:T(8,128)(2,1)S(1)} collective-permute-done((bf16[32,2560]{1,0:T(8,128)(2,1)}, bf16[32,2560]{1,0:T(8,128)(2,1)S(1)}, u32[]{:S(2)}, u32[]{:S(2)}) %collective-permute-start.27) | collective-permute-done | bytes 163872 | tf_op jit(solution)/shard_map/ppermute | solution.py:543
  312.3 5.1 %all-to-all-start = ((f32[32,1,384]{2,1,0:T(1,128)}), f32[32,1,384]{2,1,0:T(1,128)S(1)}, u32[]{:S(2)}, u32[]{:S(2)}) async-start(f32[32,1,384]{2,1,0:T(1,128)} %copy.59), calls=%async_computation | async-start | bytes 98304 | tf_op jit(solution)/shard_map/all_to_all | solution.py:890
  318.9 3.5 shard_map.312
  322.4 9.5 %all-to-all-done = f32[32,1,384]{2,1,0:T(1,128)S(1)} async-done(((f32[32,1,384]{2,1,0:T(1,128)}), f32[32,1,384]{2,1,0:T(1,128)S(1)}, u32[]{:S(2)}, u32[]{:S(2)}) %all-to-all-start) | async-done | bytes 49184 | tf_op jit(solution)/shard_map/all_to_all | solution.py:890
  332.9 5.0 %shard_map.320 = (bf16[32,3072]{1,0:T(8,128)(2,1)}, bf16[32,3072]{1,0:T(8,128)(2,1)}, bf16[32,3072]{1,0:T(8,128)(2,1)}, f32[32,3328]{1,0:T(8,128)}, f32[32,768]{...) custom-call(s32[148]{0:T(256)} %stack.115.refs_0_, ...), custom_call_target="tpu_custom_call" | custom-call | tf_op jit(solution)/shard_map/pallas_call | solution.py:56
  339.2 1.5 collective-permute-start.31
  340.7 1.7 collective-permute-start.32
  342.4 1.1 pad_maximum_fusion.1
  343.5 1.8 pad_maximum_fusion
  345.3 1.6 slice.65
  347.2 1.1 copy.60
  348.3 3.5 shard_map.319
  351.9 2.9 collective-permute-done.31.refs_6_
  354.8 5.1 %collective-permute-done.32.refs_7_ = bf16[32,3072]{1,0:T(8,128)(2,1)S(1)} collective-permute-done((bf16[32,3072]{1,0:T(8,128)(2,1)}, bf16[32,3072]{1,0:T(8,128)(2,1)S(1)}, u32[]{:S(2)}, u32[]{:S(2)}) %collective-permute-start.32) | collective-permute-done | bytes 196640 | tf_op jit(solution)/shard_map/ppermute | solution.py:543
  361.1 3.0 shard_map.321
  364.1 1.1 pad_maximum_fusion.2
  (121 shorter events, 24.9 us)
Async XLA Ops:
  0.7 5.3 %copy-start.16 = (s32[4,1024]{1,0:T(4,128)S(1)}, s32[4,1024]{1,0:T(4,128)}, u32[]{:S(2)}) copy-start(s32[4,1024]{1,0:T(4,128)} %param.21) | copy-start | bytes 49156
  3.2 11.2 %collective-permute-start.2 = (bf16[256,1024]{1,0:T(8,128)(2,1)S(1)}, bf16[256,1024]{1,0:T(8,128)(2,1)}, u32[]{:S(2)}, u32[]{:S(2)}) collective-permute-start(bf16[256,1024]{1,0:T(8,128)(2,1)S(1)} %get-tuple-element.348), channel_id=1, source_target_pairs={{0,1},{1,0},{2,3},{3,2},{4,5},{5,4},{6,7},{7,6},{8,9},{9,8},{10,11... | collective-permute-start | bytes 1572872 | tf_op jit(solution)/shard_map/ppermute | solution.py:543
  3.2 23.7 %collective-permute-start.1 = (bf16[256,1024]{1,0:T(8,128)(2,1)S(1)}, bf16[256,1024]{1,0:T(8,128)(2,1)}, u32[]{:S(2)}, u32[]{:S(2)}) collective-permute-start(bf16[256,1024]{1,0:T(8,128)(2,1)S(1)} %get-tuple-element.349), channel_id=1, source_target_pairs={{0,3},{1,2},{2,1},{3,0},{4,7},{5,6},{6,5},{7,4},{8,11},{9,10},{10,... | collective-permute-start | bytes 1572872 | tf_op jit(solution)/shard_map/ppermute | solution.py:543
  4.8 24.3 %collective-permute-start = (bf16[256,1024]{1,0:T(8,128)(2,1)S(1)}, bf16[256,1024]{1,0:T(8,128)(2,1)}, u32[]{:S(2)}, u32[]{:S(2)}) collective-permute-start(bf16[256,1024]{1,0:T(8,128)(2,1)S(1)} %get-tuple-element.350), channel_id=1, source_target_pairs={{0,2},{1,3},{2,0},{3,1},{4,6},{5,7},{6,4},{7,5},{8,10},{9,11},{10,... | collective-permute-start | bytes 1572872 | tf_op jit(solution)/shard_map/ppermute | solution.py:543
  25.0 38.2 %collective-permute-start.5 = (bf16[256,1024]{1,0:T(8,128)(2,1)}, bf16[256,1024]{1,0:T(8,128)(2,1)}, u32[]{:S(2)}, u32[]{:S(2)}) collective-permute-start(bf16[256,1024]{1,0:T(8,128)(2,1)} %get-tuple-element.344), channel_id=1, source_target_pairs={{0,3},{1,2},{2,1},{3,0},{4,7},{5,6},{6,5},{7,4},{8,11},{9,10},{10,... | collective-permute-start | bytes 1572872 | tf_op jit(solution)/shard_map/ppermute | solution.py:543
  25.8 37.4 %collective-permute-start.4 = (bf16[256,1024]{1,0:T(8,128)(2,1)}, bf16[256,1024]{1,0:T(8,128)(2,1)}, u32[]{:S(2)}, u32[]{:S(2)}) collective-permute-start(bf16[256,1024]{1,0:T(8,128)(2,1)} %get-tuple-element.345), channel_id=1, source_target_pairs={{0,2},{1,3},{2,0},{3,1},{4,6},{5,7},{6,4},{7,5},{8,10},{9,11},{10,... | collective-permute-start | bytes 1572872 | tf_op jit(solution)/shard_map/ppermute | solution.py:543
  26.6 36.7 %collective-permute-start.3 = (bf16[256,1024]{1,0:T(8,128)(2,1)}, bf16[256,1024]{1,0:T(8,128)(2,1)}, u32[]{:S(2)}, u32[]{:S(2)}) collective-permute-start(bf16[256,1024]{1,0:T(8,128)(2,1)} %get-tuple-element.346), channel_id=1, source_target_pairs={{0,1},{1,0},{2,3},{3,2},{4,5},{5,4},{6,7},{7,6},{8,9},{9,8},{10,11... | collective-permute-start | bytes 1572872 | tf_op jit(solution)/shard_map/ppermute | solution.py:543
  144.5 23.1 %collective-permute-start.6 = (bf16[256,1024]{1,0:T(8,128)(2,1)}, bf16[256,1024]{1,0:T(8,128)(2,1)}, u32[]{:S(2)}, u32[]{:S(2)}) collective-permute-start(bf16[256,1024]{1,0:T(8,128)(2,1)} %get-tuple-element.204), channel_id=1, source_target_pairs={{0,2},{1,3},{2,0},{3,1},{4,6},{5,7},{6,4},{7,5},{8,10},{9,11},{10,... | collective-permute-start | bytes 1572872 | tf_op jit(solution)/shard_map/ppermute | solution.py:543
  146.1 22.0 %collective-permute-start.7 = (bf16[256,1024]{1,0:T(8,128)(2,1)}, bf16[256,1024]{1,0:T(8,128)(2,1)}, u32[]{:S(2)}, u32[]{:S(2)}) collective-permute-start(bf16[256,1024]{1,0:T(8,128)(2,1)} %get-tuple-element.205), channel_id=1, source_target_pairs={{0,3},{1,2},{2,1},{3,0},{4,7},{5,6},{6,5},{7,4},{8,11},{9,10},{10,... | collective-permute-start | bytes 1572872 | tf_op jit(solution)/shard_map/ppermute | solution.py:543
  146.1 22.0 %collective-permute-start.9 = (bf16[512,2048]{1,0:T(8,128)(2,1)}, bf16[512,2048]{1,0:T(8,128)(2,1)}, u32[]{:S(2)}, u32[]{:S(2)}) collective-permute-start(bf16[512,2048]{1,0:T(8,128)(2,1)} %get-tuple-element.207), channel_id=1, source_target_pairs={{0,1},{1,0},{2,3},{3,2},{4,5},{5,4},{6,7},{7,6},{8,9},{9,8},{10,11... | collective-permute-start | bytes 6291464 | tf_op jit(solution)/shard_map/ppermute | solution.py:543
  146.7 21.4 %collective-permute-start.10 = (bf16[512,3072]{1,0:T(8,128)(2,1)}, bf16[512,3072]{1,0:T(8,128)(2,1)}, u32[]{:S(2)}, u32[]{:S(2)}) collective-permute-start(bf16[512,3072]{1,0:T(8,128)(2,1)} %get-tuple-element.208), channel_id=1, source_target_pairs={{0,1},{1,0},{2,3},{3,2},{4,5},{5,4},{6,7},{7,6},{8,9},{9,8},{10,11... | collective-permute-start | bytes 9437192 | tf_op jit(solution)/shard_map/ppermute | solution.py:543
  146.7 21.4 %collective-permute-start.8 = (bf16[512,4096]{1,0:T(8,128)(2,1)}, bf16[512,4096]{1,0:T(8,128)(2,1)}, u32[]{:S(2)}, u32[]{:S(2)}) collective-permute-start(bf16[512,4096]{1,0:T(8,128)(2,1)} %get-tuple-element.206), channel_id=1, source_target_pairs={{0,1},{1,0},{2,3},{3,2},{4,5},{5,4},{6,7},{7,6},{8,9},{9,8},{10,11... | collective-permute-start | bytes 12582920 | tf_op jit(solution)/shard_map/ppermute | solution.py:543
  167.5 46.2 %collective-permute-start.11 = (bf16[256,1024]{1,0:T(8,128)(2,1)}, bf16[256,1024]{1,0:T(8,128)(2,1)}, u32[]{:S(2)}, u32[]{:S(2)}) collective-permute-start(bf16[256,1024]{1,0:T(8,128)(2,1)} %get-tuple-element.225), channel_id=1, source_target_pairs={{0,1},{1,0},{2,3},{3,2},{4,5},{5,4},{6,7},{7,6},{8,9},{9,8},{10,11... | collective-permute-start | bytes 1572872 | tf_op jit(solution)/shard_map/ppermute | solution.py:543
  174.5 39.2 %collective-permute-start.14 = (bf16[256,2560]{1,0:T(8,128)(2,1)}, bf16[256,2560]{1,0:T(8,128)(2,1)}, u32[]{:S(2)}, u32[]{:S(2)}) collective-permute-start(bf16[256,2560]{1,0:T(8,128)(2,1)} %bitcast.190), channel_id=1, source_target_pairs={{0,8},{1,9},{2,10},{3,11},{4,12},{5,13},{6,14},{7,15},{8,0},{9,1},... | collective-permute-start | bytes 3932168 | tf_op jit(solution)/shard_map/ppermute | solution.py:543
  176.2 39.9 %collective-permute-start.12 = (bf16[256,3328]{1,0:T(8,128)(2,1)}, bf16[256,3328]{1,0:T(8,128)(2,1)}, u32[]{:S(2)}, u32[]{:S(2)}) collective-permute-start(bf16[256,3328]{1,0:T(8,128)(2,1)} %bitcast.189), channel_id=1, source_target_pairs={{0,4},{1,5},{2,6},{3,7},{4,0},{5,1},{6,2},{7,3},{8,12},{9,13},{10,... | collective-permute-start | bytes 5111816 | tf_op jit(solution)/shard_map/ppermute | solution.py:543
  177.7 39.6 %collective-permute-start.13 = (bf16[256,3328]{1,0:T(8,128)(2,1)}, bf16[256,3328]{1,0:T(8,128)(2,1)}, u32[]{:S(2)}, u32[]{:S(2)}) collective-permute-start(bf16[256,3328]{1,0:T(8,128)(2,1)} %bitcast.188), channel_id=1, source_target_pairs={{0,2},{1,3},{2,0},{3,1},{4,6},{5,7},{6,4},{7,5},{8,10},{9,11},{10,... | collective-permute-start | bytes 5111816 | tf_op jit(solution)/shard_map/ppermute | solution.py:543
  222.6 28.2 %collective-permute-start.17 = (bf16[128,2560]{1,0:T(8,128)(2,1)}, bf16[128,2560]{1,0:T(8,128)(2,1)}, u32[]{:S(2)}, u32[]{:S(2)}) collective-permute-start(bf16[128,2560]{1,0:T(8,128)(2,1)} %bitcast.196), channel_id=1, source_target_pairs={{0,16},{1,17},{2,18},{3,19},{4,20},{5,21},{6,22},{7,23},{8,24},{9,... | collective-permute-start | bytes 1966088 | tf_op jit(solution)/shard_map/ppermute | solution.py:543
  223.0 27.8 %collective-permute-start.15 = (bf16[128,3328]{1,0:T(8,128)(2,1)}, bf16[128,3328]{1,0:T(8,128)(2,1)}, u32[]{:S(2)}, u32[]{:S(2)}) collective-permute-start(bf16[128,3328]{1,0:T(8,128)(2,1)} %bitcast.193), channel_id=1, source_target_pairs={{0,2},{1,3},{2,0},{3,1},{4,6},{5,7},{6,4},{7,5},{8,10},{9,11},{10,... | collective-permute-start | bytes 2555912 | tf_op jit(solution)/shard_map/ppermute | solution.py:543
  224.5 26.3 %collective-permute-start.16 = (bf16[128,3328]{1,0:T(8,128)(2,1)}, bf16[128,3328]{1,0:T(8,128)(2,1)}, u32[]{:S(2)}, u32[]{:S(2)}) collective-permute-start(bf16[128,3328]{1,0:T(8,128)(2,1)} %bitcast.192), channel_id=1, source_target_pairs={{0,4},{1,5},{2,6},{3,7},{4,0},{5,1},{6,2},{7,3},{8,12},{9,13},{10,... | collective-permute-start | bytes 2555912 | tf_op jit(solution)/shard_map/ppermute | solution.py:543
  250.8 10.4 %collective-permute-start.18 = (bf16[512,3072]{1,0:T(8,128)(2,1)}, bf16[512,3072]{1,0:T(8,128)(2,1)S(1)}, u32[]{:S(2)}, u32[]{:S(2)}) collective-permute-start(bf16[512,3072]{1,0:T(8,128)(2,1)} %get-tuple-element.269), channel_id=1, source_target_pairs={{0,1},{1,0},{2,3},{3,2},{4,5},{5,4},{6,7},{7,6},{8,9},{9,8},{10,11... | collective-permute-start | bytes 9437192 | tf_op jit(solution)/shard_map/ppermute | solution.py:543
  257.0 32.0 %collective-permute-start.20 = (bf16[64,2560]{1,0:T(8,128)(2,1)}, bf16[64,2560]{1,0:T(8,128)(2,1)S(1)}, u32[]{:S(2)}, u32[]{:S(2)}) collective-permute-start(bf16[64,2560]{1,0:T(8,128)(2,1)} %bitcast.199), channel_id=1, source_target_pairs={{0,4},{1,5},{2,6},{3,7},{4,0},{5,1},{6,2},{7,3},{8,12},{9,13},{10,... | collective-permute-start | bytes 983048 | tf_op jit(solution)/shard_map/ppermute | solution.py:543
  257.7 31.2 %collective-permute-start.19 = (bf16[64,6656]{1,0:T(8,128)(2,1)}, bf16[64,6656]{1,0:T(8,128)(2,1)}, u32[]{:S(2)}, u32[]{:S(2)}) collective-permute-start(bf16[64,6656]{1,0:T(8,128)(2,1)} %bitcast.191), channel_id=1, source_target_pairs={{0,8},{1,9},{2,10},{3,11},{4,12},{5,13},{6,14},{7,15},{8,0},{9,1},... | collective-permute-start | bytes 2555912 | tf_op jit(solution)/shard_map/ppermute | solution.py:543
  261.2 1.6 copy-start
  266.3 22.7 %collective-permute-start.21 = (bf16[256,1536]{1,0:T(8,128)(2,1)}, bf16[256,1536]{1,0:T(8,128)(2,1)S(1)}, u32[]{:S(2)}, u32[]{:S(2)}) collective-permute-start(bf16[256,1536]{1,0:T(8,128)(2,1)} %bitcast.195), channel_id=1, source_target_pairs={{0,4},{1,5},{2,6},{3,7},{4,0},{5,1},{6,2},{7,3},{8,12},{9,13},{10,... | collective-permute-start | bytes 2359304 | tf_op jit(solution)/shard_map/ppermute | solution.py:543
  267.8 21.2 %collective-permute-start.22 = (bf16[256,1536]{1,0:T(8,128)(2,1)}, bf16[256,1536]{1,0:T(8,128)(2,1)S(1)}, u32[]{:S(2)}, u32[]{:S(2)}) collective-permute-start(bf16[256,1536]{1,0:T(8,128)(2,1)} %bitcast.194), channel_id=1, source_target_pairs={{0,2},{1,3},{2,0},{3,1},{4,6},{5,7},{6,4},{7,5},{8,10},{9,11},{10,... | collective-permute-start | bytes 2359304 | tf_op jit(solution)/shard_map/ppermute | solution.py:543
  289.0 1.0 copy-start.1
  289.0 1.2 copy-start.2
  290.3 21.1 %copy-start.14 = (f32[8,1024]{1,0:T(8,128)S(1)}, f32[8,1024]{1,0:T(8,128)}, u32[]{:S(2)}) copy-start(f32[8,1024]{1,0:T(8,128)} %get-tuple-element.300) | copy-start | bytes 98308
  290.3 21.3 %copy-start.15 = (f32[1,4096]{1,0:T(1,128)S(1)}, f32[1,4096]{1,0:T(1,128)}, u32[]{:S(2)}) copy-start(f32[1,4096]{1,0:T(1,128)} %get-tuple-element.301) | copy-start | bytes 49156
  294.8 15.9 %collective-permute-start.28 = (bf16[128,1536]{1,0:T(8,128)(2,1)}, bf16[128,1536]{1,0:T(8,128)(2,1)S(1)}, u32[]{:S(2)}, u32[]{:S(2)}) collective-permute-start(bf16[128,1536]{1,0:T(8,128)(2,1)} %bitcast.198), channel_id=1, source_target_pairs={{0,2},{1,3},{2,0},{3,1},{4,6},{5,7},{6,4},{7,5},{8,10},{9,11},{10,... | collective-permute-start | bytes 1179656 | tf_op jit(solution)/shard_map/ppermute | solution.py:543
  295.0 15.6 %collective-permute-start.27 = (bf16[32,2560]{1,0:T(8,128)(2,1)}, bf16[32,2560]{1,0:T(8,128)(2,1)S(1)}, u32[]{:S(2)}, u32[]{:S(2)}) collective-permute-start(bf16[32,2560]{1,0:T(8,128)(2,1)} %get-tuple-element.307), channel_id=1, source_target_pairs={{0,2},{1,3},{2,0},{3,1},{4,6},{5,7},{6,4},{7,5},{8,10},{9,11},{10,... | collective-permute-start | bytes 491528 | tf_op jit(solution)/shard_map/ppermute | solution.py:543
  296.9 35.1 %collective-permute-start.23 = (bf16[256,1024]{1,0:T(8,128)(2,1)}, bf16[256,1024]{1,0:T(8,128)(2,1)S(1)}, u32[]{:S(2)}, u32[]{:S(2)}) collective-permute-start(bf16[256,1024]{1,0:T(8,128)(2,1)} %get-tuple-element.303), channel_id=1, source_target_pairs={{0,1},{1,0},{2,3},{3,2},{4,5},{5,4},{6,7},{7,6},{8,9},{9,8},{10,11... | collective-permute-start | bytes 1572872 | tf_op jit(solution)/shard_map/ppermute | solution.py:543
  296.9 35.1 %collective-permute-start.24 = (bf16[256,1024]{1,0:T(8,128)(2,1)}, bf16[256,1024]{1,0:T(8,128)(2,1)S(1)}, u32[]{:S(2)}, u32[]{:S(2)}) collective-permute-start(bf16[256,1024]{1,0:T(8,128)(2,1)} %get-tuple-element.304), channel_id=1, source_target_pairs={{0,2},{1,3},{2,0},{3,1},{4,6},{5,7},{6,4},{7,5},{8,10},{9,11},{10,... | collective-permute-start | bytes 1572872 | tf_op jit(solution)/shard_map/ppermute | solution.py:543
  297.1 35.0 %collective-permute-start.25 = (bf16[256,1024]{1,0:T(8,128)(2,1)}, bf16[256,1024]{1,0:T(8,128)(2,1)S(1)}, u32[]{:S(2)}, u32[]{:S(2)}) collective-permute-start(bf16[256,1024]{1,0:T(8,128)(2,1)} %get-tuple-element.305), channel_id=1, source_target_pairs={{0,3},{1,2},{2,1},{3,0},{4,7},{5,6},{6,5},{7,4},{8,11},{9,10},{10,... | collective-permute-start | bytes 1572872 | tf_op jit(solution)/shard_map/ppermute | solution.py:543
  310.7 11.8 %copy-start.13 = (bf16[32,2560]{1,0:T(8,128)(2,1)}, bf16[32,2560]{1,0:T(8,128)(2,1)S(1)}, u32[]{:S(2)}) copy-start(bf16[32,2560]{1,0:T(8,128)(2,1)S(1)} %collective-permute-done.27.refs_22_) | copy-start | bytes 491524
  310.7 21.3 %collective-permute-start.26 = (bf16[32,6656]{1,0:T(8,128)(2,1)}, bf16[32,6656]{1,0:T(8,128)(2,1)S(1)}, u32[]{:S(2)}, u32[]{:S(2)}) collective-permute-start(bf16[32,6656]{1,0:T(8,128)(2,1)} %get-tuple-element.306), channel_id=1, source_target_pairs={{0,16},{1,17},{2,18},{3,19},{4,20},{5,21},{6,22},{7,23},{8,24},{9,... | collective-permute-start | bytes 1277960 | tf_op jit(solution)/shard_map/ppermute | solution.py:543
  310.7 11.8 %copy-start.3 = (bf16[128,1536]{1,0:T(8,128)(2,1)}, bf16[128,1536]{1,0:T(8,128)(2,1)S(1)}, u32[]{:S(2)}) copy-start(bf16[128,1536]{1,0:T(8,128)(2,1)S(1)} %collective-permute-done.28) | copy-start | bytes 1179652
  310.7 21.3 %collective-permute-start.29 = (bf16[128,1536]{1,0:T(8,128)(2,1)}, bf16[128,1536]{1,0:T(8,128)(2,1)S(1)}, u32[]{:S(2)}, u32[]{:S(2)}) collective-permute-start(bf16[128,1536]{1,0:T(8,128)(2,1)} %bitcast.197), channel_id=1, source_target_pairs={{0,4},{1,5},{2,6},{3,7},{4,0},{5,1},{6,2},{7,3},{8,12},{9,13},{10,... | collective-permute-start | bytes 1179656 | tf_op jit(solution)/shard_map/ppermute | solution.py:543
  312.3 19.7 %all-to-all-start = ((f32[32,1,384]{2,1,0:T(1,128)}), f32[32,1,384]{2,1,0:T(1,128)S(1)}, u32[]{:S(2)}, u32[]{:S(2)}) async-start(f32[32,1,384]{2,1,0:T(1,128)} %copy.59), calls=%async_computation | async-start | bytes 98304 | tf_op jit(solution)/shard_map/all_to_all | solution.py:890
  332.0 5.8 %copy-start.6 = (bf16[256,1024]{1,0:T(8,128)(2,1)}, bf16[256,1024]{1,0:T(8,128)(2,1)S(1)}, u32[]{:S(2)}) copy-start(bf16[256,1024]{1,0:T(8,128)(2,1)S(1)} %collective-permute-done.23.refs_1_) | copy-start | bytes 1572868
  332.0 5.8 %copy-start.7 = (bf16[256,1024]{1,0:T(8,128)(2,1)}, bf16[256,1024]{1,0:T(8,128)(2,1)S(1)}, u32[]{:S(2)}) copy-start(bf16[256,1024]{1,0:T(8,128)(2,1)S(1)} %collective-permute-done.24.refs_2_) | copy-start | bytes 1572868
  332.1 5.8 %copy-start.8 = (bf16[256,1024]{1,0:T(8,128)(2,1)}, bf16[256,1024]{1,0:T(8,128)(2,1)S(1)}, u32[]{:S(2)}) copy-start(bf16[256,1024]{1,0:T(8,128)(2,1)S(1)} %collective-permute-done.25.refs_3_) | copy-start | bytes 1572868
  338.8 13.0 %collective-permute-start.30 = (bf16[32,3072]{1,0:T(8,128)(2,1)}, bf16[32,3072]{1,0:T(8,128)(2,1)S(1)}, u32[]{:S(2)}, u32[]{:S(2)}) collective-permute-start(bf16[32,3072]{1,0:T(8,128)(2,1)} %get-tuple-element.323), channel_id=1, source_target_pairs={{0,8},{1,9},{2,10},{3,11},{4,12},{5,13},{6,14},{7,15},{8,0},{9,1},... | collective-permute-start | bytes 589832 | tf_op jit(solution)/shard_map/ppermute | solution.py:543
  339.2 15.6 %collective-permute-start.31 = (bf16[32,3072]{1,0:T(8,128)(2,1)}, bf16[32,3072]{1,0:T(8,128)(2,1)S(1)}, u32[]{:S(2)}, u32[]{:S(2)}) collective-permute-start(bf16[32,3072]{1,0:T(8,128)(2,1)} %get-tuple-element.324), channel_id=1, source_target_pairs={{0,16},{1,17},{2,18},{3,19},{4,20},{5,21},{6,22},{7,23},{8,24},{9,... | collective-permute-start | bytes 589832 | tf_op jit(solution)/shard_map/ppermute | solution.py:543
  340.7 19.2 %collective-permute-start.32 = (bf16[32,3072]{1,0:T(8,128)(2,1)}, bf16[32,3072]{1,0:T(8,128)(2,1)S(1)}, u32[]{:S(2)}, u32[]{:S(2)}) collective-permute-start(bf16[32,3072]{1,0:T(8,128)(2,1)} %get-tuple-element.325), channel_id=1, source_target_pairs={{0,24},{1,25},{2,26},{3,27},{4,28},{5,29},{6,30},{7,31},{8,16},{9,... | collective-permute-start | bytes 589832 | tf_op jit(solution)/shard_map/ppermute | solution.py:543
  351.9 9.2 %copy-start.10 = (bf16[32,3072]{1,0:T(8,128)(2,1)}, bf16[32,3072]{1,0:T(8,128)(2,1)S(1)}, u32[]{:S(2)}) copy-start(bf16[32,3072]{1,0:T(8,128)(2,1)S(1)} %collective-permute-done.30.refs_5_) | copy-start | bytes 589828
  354.8 6.3 %copy-start.11 = (bf16[32,3072]{1,0:T(8,128)(2,1)}, bf16[32,3072]{1,0:T(8,128)(2,1)S(1)}, u32[]{:S(2)}) copy-start(bf16[32,3072]{1,0:T(8,128)(2,1)S(1)} %collective-permute-done.31.refs_6_) | copy-start | bytes 589828
  359.9 1.2 copy-start.12
  (3 other events, 2.4 us)
